TPU v7x, 32 devices: a whole 2x2x4 slice. The times are simulated.
32 devices in a mesh: gx: 4 (over y, x), gy: 4 (over z), gz: 2 (over core).
Axes of the slice: x: 2, y: 2, z: 4, core: 2. Of those that a mesh axis runs over, the one named last changes fastest.
Arguments:
- orbitals: float32 [8, 64, 64, 256], P(None, 'gx', 'gy', 'gz'), may hold values from -7 to 7
- potential: float32 [64, 64, 256], P('gx', 'gy', 'gz'), may hold values from -2 to 1
- locked: bfloat16 [64, 64, 64, 256], P(None, 'gx', 'gy', 'gz'), may hold values from -160 to 160
- sphere_cell: int32 [4, 4, 2, 16384], P('gx', 'gy', 'gz'), may hold values from 0 to 32767
- sphere_owner: int32 [4, 4, 2, 16384], P('gx', 'gy', 'gz'), may hold values from 0 to 26
- sphere_atom: int32 [4, 4, 2, 16384], P('gx', 'gy', 'gz'), may hold values from 0 to 31
- sphere_profile: float32 [4, 4, 2, 9, 16384], P('gx', 'gy', 'gz'), may hold values from -1.2 to 1.2
- atom_strength: float32 [4, 4, 2, 32, 9], P('gx', 'gy', 'gz'), may hold values from -0.5 to 2
- atom_channels: int32 [4, 4, 2, 32], P('gx', 'gy', 'gz'), may hold values from 0 to 9, as said below
Outputs:
- projected: float32 [8, 64, 64, 256], P(None, 'gx', 'gy', 'gz')
Inputs may be any that keep to these rules, and one draw needn't show every extreme that they name: `sphere_owner`: A code o stands for the domain (e, f, g) steps away along the three axes, o = 9 (e + 1) + 3 (f + 1) + (g + 1), with the grid's ends joined; every code occurs. `atom_channels`: each entry is 0, 1, 4 or 9; the first slot of every domain has 9.
All inputs are finite; a program needn't handle non-finite values.
Results may differ from a plain program's by a relative error of at most 0.0018.
Values sent between devices are 32-bit elements; how exact they have to be, the bound alone decides.
No kernel may reach another device: no remote copies, remote signals or barrier semaphores. Data moves between devices by JAX's collectives and lax.ppermute only.
A program may use at most 128 MiB of HBM per device.

v0:
```python
import jax
import jax.numpy as jnp
from jax import lax
from jax.sharding import PartitionSpec as P

STENCIL_WEIGHTS = (-205.0 / 72.0, 8.0 / 5.0, -1.0 / 5.0, 8.0 / 315.0, -1.0 / 560.0)


def extended_2(block, sides, width):
    for axis, dim in sides:
        count = lax.axis_size(axis)
        forward = [(i, i + 1) for i in range(count - 1)]
        forward.append((count - 1, 0))
        backward = [(target, source) for source, target in forward]
        low = lax.ppermute(
            lax.slice_in_dim(block, block.shape[dim] - width, None, axis=dim), axis, forward
        )
        high = lax.ppermute(lax.slice_in_dim(block, 0, width, axis=dim), axis, backward)
        block = jnp.concatenate([low, block, high], axis=dim)
    return block


def slot_onehot(owners, atom_ids, atom_slots):
    slot_ids = owners * atom_slots + atom_ids
    labels = jnp.arange(27 * atom_slots, dtype=jnp.int32)
    return (labels[:, None] == slot_ids[None, :]).astype(jnp.float32)


def gather_slots(flat_orbitals, cell_index, onehot, profile):
    values = jnp.take(flat_orbitals, cell_index, axis=1)
    products = (profile[:, None, :] * values[None, :, :]).reshape(-1, cell_index.shape[0])
    return lax.dot_general(
        onehot,
        products,
        (((1,), (1,)), ((), ())),
        precision=lax.Precision.HIGHEST,
        preferred_element_type=jnp.float32,
    )


def spread_terms(returned, cell_index, onehot, profile, orbit_count, cell_count):
    picked = lax.dot_general(
        returned,
        onehot,
        (((0,), (0,)), ((), ())),
        precision=lax.Precision.HIGHEST,
        preferred_element_type=jnp.float32,
    )
    picked = picked.reshape(profile.shape[0], orbit_count, cell_index.shape[0])
    spread = jnp.sum(profile[:, None, :] * picked, axis=0)
    return jnp.zeros((orbit_count, cell_count), jnp.float32).at[:, cell_index].add(spread)


def locked_solve(gram_matrix, correlation):
    factor = jnp.linalg.cholesky(gram_matrix)
    middle = lax.linalg.triangular_solve(factor, correlation, left_side=True, lower=True)
    return lax.linalg.triangular_solve(factor, middle, left_side=True, lower=True, transpose_a=True)


def line_terms(extended, dimension, length):
    summed = None
    for distance in range(1, 5):
        forward = lax.slice_in_dim(extended, 4 + distance, 4 + distance + length, axis=dimension)
        backward = lax.slice_in_dim(extended, 4 - distance, 4 - distance + length, axis=dimension)
        paired = STENCIL_WEIGHTS[distance] * (forward + backward)
        summed = paired if summed is None else summed + paired
    return summed


def on_device(
    orbitals,
    potential,
    locked,
    sphere_cell,
    sphere_owner,
    sphere_atom,
    sphere_profile,
    atom_strength,
    atom_channels,
):
    orbit_count, span_one, span_two, span_three = orbitals.shape
    cell_count = span_one * span_two * span_three
    locked_count = locked.shape[0]
    locked_flat = locked.reshape(locked_count, cell_count)
    gram_local = lax.dot_general(
        locked_flat, locked_flat, (((1,), (1,)), ((), ())), preferred_element_type=jnp.float32
    )
    padded = extended_2(orbitals, (("gx", 1), ("gy", 2), ("gz", 3)), 4)
    along_one = padded[:, :, 4 : 4 + span_two, 4 : 4 + span_three]
    along_two = padded[:, 4 : 4 + span_one, :, 4 : 4 + span_three]
    along_three = padded[:, 4 : 4 + span_one, 4 : 4 + span_two, :]
    laplace = 3.0 * STENCIL_WEIGHTS[0] * orbitals
    laplace = laplace + line_terms(along_one, 1, span_one)
    laplace = laplace + line_terms(along_two, 2, span_two)
    laplace = laplace + line_terms(along_three, 3, span_three)
    local_part = -0.5 * laplace + potential[None] * orbitals
    atom_slots = atom_channels.shape[3]
    channel_count = sphere_profile.shape[3]
    point_count = sphere_cell.shape[3]
    cell_index = sphere_cell.reshape(point_count)
    onehot = slot_onehot(
        sphere_owner.reshape(point_count), sphere_atom.reshape(point_count), atom_slots
    )
    profile = sphere_profile.reshape(channel_count, point_count)
    flat_orbitals = orbitals.reshape(orbit_count, cell_count)
    slot_sums = gather_slots(flat_orbitals, cell_index, onehot, profile)
    surrounded = extended_2(slot_sums.reshape(3, 3, 3, -1), (("gx", 0), ("gy", 1), ("gz", 2)), 1)
    coefficient = jnp.sum(surrounded[0::2, 0::2, 0::2].reshape(27, -1), axis=0)
    active = (
        jnp.arange(channel_count, dtype=jnp.int32)[None, :]
        < atom_channels.reshape(atom_slots)[:, None]
    )
    strength = jnp.where(active, atom_strength.reshape(atom_slots, channel_count), 0.0)
    weighted = coefficient.reshape(atom_slots, channel_count, orbit_count) * strength[:, :, None]
    returned = extended_2(weighted.reshape(1, 1, 1, -1), (("gx", 0), ("gy", 1), ("gz", 2)), 1)
    nonlocal_part = spread_terms(
        returned.reshape(27 * atom_slots, channel_count * orbit_count),
        cell_index,
        onehot,
        profile,
        orbit_count,
        cell_count,
    )
    applied = local_part + nonlocal_part.reshape(orbit_count, span_one, span_two, span_three)
    rounded = applied.astype(jnp.bfloat16).reshape(orbit_count, cell_count)
    correlation_local = lax.dot_general(
        locked_flat, rounded, (((1,), (1,)), ((), ())), preferred_element_type=jnp.float32
    )
    gram_matrix, correlation = lax.psum((gram_local, correlation_local), ("gx", "gy", "gz"))
    mixing = locked_solve(gram_matrix, correlation).astype(jnp.bfloat16)
    correction = lax.dot_general(
        mixing, locked_flat, (((0,), (0,)), ((), ())), preferred_element_type=jnp.float32
    )
    return applied - correction.reshape(orbit_count, span_one, span_two, span_three)


def solution(mesh):
    placed = (
        P(None, "gx", "gy", "gz"),
        P("gx", "gy", "gz"),
        P(None, "gx", "gy", "gz"),
        P("gx", "gy", "gz", None),
        P("gx", "gy", "gz", None),
        P("gx", "gy", "gz", None),
        P("gx", "gy", "gz", None, None),
        P("gx", "gy", "gz", None, None),
        P("gx", "gy", "gz", None),
    )
    return jax.shard_map(
        on_device, mesh=mesh, in_specs=placed, out_specs=P(None, "gx", "gy", "gz"), check_vma=False
    )
```

profile of v0, /device:TPU:0, one launch (start us, length us, event | category | flops | bytes accessed | tf_op | source)
XLA Modules:
  0.0 422.4 jit_solution(12868667081959959381)
XLA Ops:
  1.6 9.9 %copy.58 = f32[8,16,16,128]{0,3,2,1:T(8,128)} copy(f32[8,16,16,128]{3,2,1,0:T(8,128)} %param.9) | data formatting | bytes 2097152 | tf_op args[0]
  11.4 60.6 %gather_fusion = f32[16384,8]{1,0:T(8,128)} fusion(f32[8,32768]{0,1:T(8,128)} %bitcast.70, s32[16384]{0:T(1024)S(1)} %broadcast_clamp_fusion), kind=kCustom, calls=%fused_computation | custom fusion | bytes 1114112 | tf_op jit(solution)/shard_map/jit(_take)/gather | solution.py:30
  72.0 13.2 %select_bitcast_fusion = f32[8,16384]{0,1:T(8,128)} fusion(f32[16384,8]{1,0:T(8,128)} %gather_fusion, pred[16384]{0:T(1024)(128)(4,1)S(1)} %compare_and_fusion), kind=kLoop, calls=%fused_computation.9 | loop fusion | flops 131072 | bytes 1064960 | tf_op jit(solution)/shard_map/jit(_take)/select_n | solution.py:30
  85.2 5.6 %copy.59 = f32[8,16384]{1,0:T(8,128)S(1)} copy(f32[8,16384]{0,1:T(8,128)} %select_bitcast_fusion) | data formatting | bytes 1048576 | tf_op jit(solution)/shard_map/jit(_take)/select_n | solution.py:30
  91.4 36.5 %fusion.1 = f32[864,72]{0,1:T(8,128)S(1)} fusion(s32[16384]{0:T(1024)S(1)} %bitcast.80, f32[8,16384]{1,0:T(8,128)S(1)} %copy.59, f32[9,16384]{1,0:T(8,128)S(1)} %bitcast.74), kind=kOutput, calls=%fused_computation.4 | convolution fusion | flops 12245925888 | bytes 1428480 | tf_op jit(solution)/shard_map/dot_general | solution.py:32
  128.2 3.0 collective-permute-start.6
  131.5 1.0 collective-permute-start.7
  132.8 1.1 collective-permute-start.1
  134.7 1.9 collective-permute-start
  137.3 1.7 collective-permute-done.7
  139.1 1.6 collective-permute-start.8
  140.7 2.3 collective-permute-start.9
  143.4 4.2 collective-permute-done.8
  147.5 1.2 collective-permute-done.9
  149.7 1.9 constant_dynamic-update-slice_fusion.1
  151.7 1.2 copy-done.3
  152.8 1.9 pad_maximum_fusion.1
  154.7 4.7 %slice.211 = f32[3,3,3,2304]{3,2,1,0:T(4,128)S(1)} slice(f32[5,5,5,2304]{3,2,1,0:T(8,128)} %pad_maximum_fusion.1), slice={[0:5:2], [0:5:2], [0:5:2], [0:2304:1]} | slice | bytes 497664 | tf_op jit(solution)/shard_map/slice | solution.py:108
  159.5 1.8 collective-permute-start.12
  161.3 1.2 collective-permute-start.13
  162.5 1.7 constant_dynamic-update-slice_fusion
  165.0 1.2 collective-permute-start.14
  166.2 2.7 collective-permute-start.15
  168.9 2.1 fusion.80
  171.5 1.5 collective-permute-start.3
  173.6 8.4 %fusion.27 = f32[64,64]{0,1:T(8,128)S(1)} fusion(bf16[64,16,16,128]{3,2,1,0:T(8,128)(2,1)} %param.11), kind=kOutput, calls=%fused_computation.39 | convolution fusion | flops 268435456 | bytes 4210688 | tf_op jit(solution)/shard_map/dot_general | solution.py:85
  182.1 2.7 copy.106
  184.8 3.1 copy.84
  187.9 1.0 pad_maximum_fusion.10
  188.9 1.4 reshape.165
  191.3 1.6 pad_maximum_fusion
  192.9 3.0 fusion.79
  195.9 2.9 copy.53
  198.9 3.6 copy.55
  203.0 23.8 %fusion.21 = f32[8,16384]{1,0:T(8,128)} fusion(s32[16384]{0:T(1024)S(1)} %bitcast.81, f32[9,16384]{1,0:T(8,128)} %bitcast.75, f32[72,864]{1,0:T(8,128)} %copy.64), kind=kOutput, calls=%fused_computation.37 | convolution fusion | flops 12246974464 | bytes 1428480 | tf_op jit(solution)/shard_map/dot_general | solution.py:42
  226.9 5.7 %copy.65 = f32[16384,8]{1,0:T(8,128)} copy(f32[16384,8]{0,1:T(8,128)} %bitcast.76) | data formatting | bytes 1048576 | tf_op jit(solution)/shard_map/reduce_sum | solution.py:50
  232.6 94.5 %scatter_custom_fusion = f32[8,32768]{0,1:T(8,128)} fusion(s32[16384]{0:T(1024)} %bitcast.79, f32[16384,8]{1,0:T(8,128)} %copy.65, f32[]{:T(128)} %constant.70.clone.1), kind=kCustom, calls=%fused_computation.10 | custom fusion | flops 131072 | bytes 1049088 | tf_op jit(solution)/shard_map/scatter-add | solution.py:51
  327.1 10.6 %copy.67 = f32[8,16,16,128]{3,0,2,1:T(8,128)} copy(f32[8,16,16,128]{0,3,2,1:T(8,128)} %bitcast.69) | data formatting | bytes 2097152 | tf_op jit(solution)/shard_map/reshape | solution.py:124
  337.7 3.7 copy.54
  341.4 3.6 copy.56
  345.0 15.3 %fusion.43 = f32[8,16,16,128]{3,0,2,1:T(8,128)S(1)} fusion(f32[8,16,16,128]{3,0,2,1:T(8,128)} %copy.67, f32[8,24,16,128]{3,0,2,1:T(8,128)} %get-tuple-element.21, f32[8,24,4,128]{3,0,2,1:T(8,128)} %collective-permute-done.3, f32[8,24,4,128]{3,0,2,1:T(8,128)S(1)} %collective-permute-done.2, f32[8,24,24,4]{3,0,2,1:T(8,128)} %copy.56, ...), kind=kLoop, calls=%fused_computation.52 | loop fusion | flops 19136512 | bytes 14172160 | tf_op jit(solution)/shard_map/add | solution.py:124
  360.3 1.0 copy-done.4
  361.3 3.5 fusion.30
  364.8 38.9 %all-reduce = (f32[64,8]{0,1:T(8,128)S(1)}, f32[64,64]{0,1:T(8,128)S(1)}) all-reduce(f32[64,8]{0,1:T(8,128)S(1)} %fusion.30, f32[64,64]{0,1:T(8,128)S(1)} %fusion.27), channel_id=1, replica_groups=mesh['gx'=4,'gy'=4,'gz'=2] {'gx','gy','gz'}, use_global_device_ids=true, to_apply=%region_6.7 | all-reduce | flops 4608 | bytes 36864 | tf_op jit(solution)/shard_map/psum | solution.py:129
  403.7 5.8 %cholesky.16 = f32[64,64]{1,0:T(8,128)S(1)} custom-call(f32[64,64]{1,0:T(8,128)S(1)} %fusion.78), custom_call_target="Cholesky" | custom-call | tf_op jit(solution)/shard_map/jit(cholesky)/cholesky | solution.py:55
  410.9 4.9 %custom-call.8 = f32[1,64,64]{1,2,0:T(8,128)S(1)} custom-call(f32[1,64,64]{2,1,0:T(8,128)S(1)} %fusion.74), custom_call_target="InvertDiagBlocksLowerTriangular" | custom-call | tf_op jit(solution)/shard_map/triangular_solve | solution.py:57
  416.1 4.9 %fusion.24 = f32[8,16,16,128]{3,0,2,1:T(8,128)S(1)} fusion(f32[8,16,16,128]{3,0,2,1:T(8,128)} %copy-done.4, bf16[64,8,1,1]{0,1,3,2:T(8,128)(2,1)S(1)} %fusion.33, bf16[16,16,128,64]{2,1,0,3:T(8,128)(2,1)} %bitcast.72), kind=kOutput, calls=%fused_computation.38 | convolution fusion | flops 33816576 | bytes 6292480 | tf_op jit(solution)/shard_map/dot_general | solution.py:131
  420.9 1.2 copy.74
  (89 shorter events, 11.0 us)
Async XLA Ops:
  0.9 0.6 copy-start.8
  1.5 9.9 %copy-start.7 = (s32[1,1,1,16384]{3,2,1,0:T(1,128)S(1)}, s32[1,1,1,16384]{3,2,1,0:T(1,128)}, u32[]{:S(2)}) copy-start(s32[1,1,1,16384]{3,2,1,0:T(1,128)} %param.12) | copy-start | bytes 196612
  85.2 5.6 %copy-start.6 = (f32[1,1,1,9,16384]{4,2,3,1,0:T(1,128)S(1)}, f32[1,1,1,9,16384]{4,2,3,1,0:T(1,128)}, u32[]{:S(2)}) copy-start(f32[1,1,1,9,16384]{4,2,3,1,0:T(1,128)} %param.15) | copy-start | bytes 1769476
  85.2 6.0 %copy-start.10 = (s32[1,1,1,16384]{3,2,1,0:T(1,128)S(1)}, s32[1,1,1,16384]{3,2,1,0:T(1,128)}, u32[]{:S(2)}) copy-start(s32[1,1,1,16384]{3,2,1,0:T(1,128)} %param.14) | copy-start | bytes 196612
  85.2 6.0 %copy-start.11 = (s32[1,1,1,16384]{3,2,1,0:T(1,128)S(1)}, s32[1,1,1,16384]{3,2,1,0:T(1,128)}, u32[]{:S(2)}) copy-start(s32[1,1,1,16384]{3,2,1,0:T(1,128)} %param.13) | copy-start | bytes 196612
  91.2 36.6 %copy-start.5 = (f32[1,1,1,9,16384]{4,3,2,1,0:T(8,128)}, f32[1,1,1,9,16384]{4,3,2,1,0:T(8,128)S(1)}, u32[]{:S(2)}) copy-start(f32[1,1,1,9,16384]{4,3,2,1,0:T(8,128)S(1)} %copy.107) | copy-start | bytes 1769476
  91.3 36.5 %copy-start.12 = (s32[1,1,1,16384]{3,2,1,0:T(1,128)}, s32[1,1,1,16384]{3,2,1,0:T(1,128)S(1)}, u32[]{:S(2)}) copy-start(s32[1,1,1,16384]{3,2,1,0:T(1,128)S(1)} %multiply_add_fusion) | copy-start | bytes 196612
  91.3 41.2 %copy-start.2 = (f32[8,16,16,128]{3,2,1,0:T(8,128)S(1)}, f32[8,16,16,128]{3,2,1,0:T(8,128)}, u32[]{:S(2)}) copy-start(f32[8,16,16,128]{3,2,1,0:T(8,128)} %param.9) | copy-start | bytes 3145732
  128.2 9.0 %collective-permute-start.6 = (f32[1,3,3,2304]{3,2,1,0:T(4,128)S(1)}, f32[1,3,3,2304]{3,2,1,0:T(4,128)S(1)}, u32[]{:S(2)}, u32[]{:S(2)}) collective-permute-start(f32[1,3,3,2304]{3,2,1,0:T(4,128)S(1)} %slice.204), channel_id=1, source_target_pairs={{0,8},{8,16},{16,24},{24,0},{1,9},{9,17},{17,25},{25,1},{2,10},{10... | collective-permute-start | bytes 248840 | tf_op jit(solution)/shard_map/ppermute | solution.py:15
  131.5 7.5 %collective-permute-start.7 = (f32[1,3,3,2304]{3,2,1,0:T(4,128)S(1)}, f32[1,3,3,2304]{3,2,1,0:T(4,128)S(1)}, u32[]{:S(2)}, u32[]{:S(2)}) collective-permute-start(f32[1,3,3,2304]{3,2,1,0:T(4,128)S(1)} %slice.206), channel_id=1, source_target_pairs={{8,0},{16,8},{24,16},{0,24},{9,1},{17,9},{25,17},{1,25},{10,2},{18... | collective-permute-start | bytes 248840 | tf_op jit(solution)/shard_map/ppermute | solution.py:18
  132.6 10.4 %copy-start.14 = (f32[1,1,1,32,9]{3,2,4,1,0:T(1,128)S(1)}, f32[1,1,1,32,9]{3,2,4,1,0:T(1,128)}, u32[]{:S(2)}) copy-start(f32[1,1,1,32,9]{3,2,4,1,0:T(1,128)} %param.16) | copy-start | bytes 3460
  132.6 10.4 %copy-start.15 = (s32[1,1,1,32]{3,2,1,0:T(1,128)S(1)}, s32[1,1,1,32]{3,2,1,0:T(1,128)}, u32[]{:S(2)}) copy-start(s32[1,1,1,32]{3,2,1,0:T(1,128)} %param.17) | copy-start | bytes 388
  132.8 17.0 %collective-permute-start.1 = (f32[8,4,16,128]{3,0,2,1:T(8,128)S(1)}, f32[8,4,16,128]{3,0,2,1:T(8,128)S(1)}, u32[]{:S(2)}, u32[]{:S(2)}) collective-permute-start(f32[8,4,16,128]{3,0,2,1:T(8,128)S(1)} %copy.104), channel_id=1, source_target_pairs={{0,8},{8,16},{16,24},{24,0},{1,9},{9,17},{17,25},{25,1},{2,10},{10... | collective-permute-start | bytes 786440 | tf_op jit(solution)/shard_map/ppermute | solution.py:15
  134.7 27.8 %collective-permute-start = (f32[8,4,16,128]{3,0,2,1:T(8,128)}, f32[8,4,16,128]{3,0,2,1:T(8,128)}, u32[]{:S(2)}, u32[]{:S(2)}) collective-permute-start(f32[8,4,16,128]{3,0,2,1:T(8,128)} %copy.105), channel_id=1, source_target_pairs={{8,0},{16,8},{24,16},{0,24},{9,1},{17,9},{25,17},{1,25},{10,2},{18... | collective-permute-start | bytes 786440 | tf_op jit(solution)/shard_map/ppermute | solution.py:18
  139.1 8.4 %collective-permute-start.8 = (f32[5,1,3,2304]{3,2,1,0:T(4,128)S(1)}, f32[5,1,3,2304]{3,2,1,0:T(4,128)S(1)}, u32[]{:S(2)}, u32[]{:S(2)}) collective-permute-start(f32[5,1,3,2304]{3,2,1,0:T(4,128)S(1)} %get-tuple-element.18), channel_id=1, source_target_pairs={{0,2},{2,4},{4,6},{6,0},{1,3},{3,5},{5,7},{7,1},{8,10},{10,12},{12... | collective-permute-start | bytes 414728 | tf_op jit(solution)/shard_map/ppermute | solution.py:15
  140.7 8.0 %collective-permute-start.9 = (f32[5,1,3,2304]{3,2,1,0:T(4,128)S(1)}, f32[5,1,3,2304]{3,2,1,0:T(4,128)S(1)}, u32[]{:S(2)}, u32[]{:S(2)}) collective-permute-start(f32[5,1,3,2304]{3,2,1,0:T(4,128)S(1)} %get-tuple-element.19), channel_id=1, source_target_pairs={{2,0},{4,2},{6,4},{0,6},{3,1},{5,3},{7,5},{1,7},{10,8},{12,10},{14... | collective-permute-start | bytes 414728 | tf_op jit(solution)/shard_map/ppermute | solution.py:18
  149.1 3.7 collective-permute-start.10
  149.2 3.6 collective-permute-start.11
  151.7 1.2 copy-start.3
  159.5 4.7 %collective-permute-start.12 = (f32[1,1,1,2304]{3,2,1,0:T(1,128)S(1)}, f32[1,1,1,2304]{3,2,1,0:T(1,128)S(1)}, u32[]{:S(2)}, u32[]{:S(2)}) collective-permute-start(f32[1,1,1,2304]{3,2,1,0:T(1,128)S(1)} %reshape_multiply_fusion), channel_id=1, source_target_pairs={{0,8},{8,16},{16,24},{24,0},{1,9},{9,17},{17,25},{25,1},{2,10},{10... | collective-permute-start | bytes 27656 | tf_op jit(solution)/shard_map/ppermute | solution.py:15
  161.3 3.7 collective-permute-start.13
  165.0 8.0 %collective-permute-start.14 = (f32[3,1,1,2304]{3,2,1,0:T(1,128)S(1)}, f32[3,1,1,2304]{3,2,1,0:T(1,128)S(1)}, u32[]{:S(2)}, u32[]{:S(2)}) collective-permute-start(f32[3,1,1,2304]{3,2,1,0:T(1,128)S(1)} %pad_maximum_fusion.15), channel_id=1, source_target_pairs={{0,2},{2,4},{4,6},{6,0},{1,3},{3,5},{5,7},{7,1},{8,10},{10,12},{12... | collective-permute-start | bytes 82952 | tf_op jit(solution)/shard_map/ppermute | solution.py:15
  166.2 6.8 %collective-permute-start.15 = (f32[3,1,1,2304]{3,2,1,0:T(1,128)S(1)}, f32[3,1,1,2304]{3,2,1,0:T(1,128)S(1)}, u32[]{:S(2)}, u32[]{:S(2)}) collective-permute-start(f32[3,1,1,2304]{3,2,1,0:T(1,128)S(1)} %pad_maximum_fusion.15), channel_id=1, source_target_pairs={{2,0},{4,2},{6,4},{0,6},{3,1},{5,3},{7,5},{1,7},{10,8},{12,10},{14... | collective-permute-start | bytes 82952 | tf_op jit(solution)/shard_map/ppermute | solution.py:18
  170.9 20.3 %collective-permute-start.2 = (f32[8,24,4,128]{3,0,2,1:T(8,128)}, f32[8,24,4,128]{3,0,2,1:T(8,128)S(1)}, u32[]{:S(2)}, u32[]{:S(2)}) collective-permute-start(f32[8,24,4,128]{3,0,2,1:T(8,128)} %get-tuple-element.9), channel_id=1, source_target_pairs={{2,0},{4,2},{6,4},{0,6},{3,1},{5,3},{7,5},{1,7},{10,8},{12,10},{14... | collective-permute-start | bytes 1179656 | tf_op jit(solution)/shard_map/ppermute | solution.py:18
  171.5 19.8 %collective-permute-start.3 = (f32[8,24,4,128]{3,0,2,1:T(8,128)}, f32[8,24,4,128]{3,0,2,1:T(8,128)}, u32[]{:S(2)}, u32[]{:S(2)}) collective-permute-start(f32[8,24,4,128]{3,0,2,1:T(8,128)} %get-tuple-element.10), channel_id=1, source_target_pairs={{0,2},{2,4},{4,6},{6,0},{1,3},{3,5},{5,7},{7,1},{8,10},{10,12},{12... | collective-permute-start | bytes 1179656 | tf_op jit(solution)/shard_map/ppermute | solution.py:15
  173.1 9.0 %copy-start = (bf16[64,16,16,128]{3,2,1,0:T(8,128)(2,1)S(1)}, bf16[64,16,16,128]{3,2,1,0:T(8,128)(2,1)}, u32[]{:S(2)}) copy-start(bf16[64,16,16,128]{3,2,1,0:T(8,128)(2,1)} %param.11) | copy-start | bytes 12582916
  173.1 14.9 %collective-permute-start.16 = (f32[3,3,1,2304]{3,2,1,0:T(1,128)S(1)}, f32[3,3,1,2304]{3,2,1,0:T(1,128)S(1)}, u32[]{:S(2)}, u32[]{:S(2)}) collective-permute-start(f32[3,3,1,2304]{3,2,1,0:T(1,128)S(1)} %pad_maximum_fusion.14), channel_id=1, source_target_pairs={{0,1},{1,0},{2,3},{3,2},{4,5},{5,4},{6,7},{7,6},{8,9},{9,8},{10,11... | collective-permute-start | bytes 248840 | tf_op jit(solution)/shard_map/ppermute | solution.py:15
  173.1 14.8 %collective-permute-start.17 = (f32[3,3,1,2304]{3,2,1,0:T(1,128)S(1)}, f32[3,3,1,2304]{3,2,1,0:T(1,128)S(1)}, u32[]{:S(2)}, u32[]{:S(2)}) collective-permute-start(f32[3,3,1,2304]{3,2,1,0:T(1,128)S(1)} %pad_maximum_fusion.14), channel_id=1, source_target_pairs={{1,0},{0,1},{3,2},{2,3},{5,4},{4,5},{7,6},{6,7},{9,8},{8,9},{11,10... | collective-permute-start | bytes 248840 | tf_op jit(solution)/shard_map/ppermute | solution.py:18
  195.9 7.1 %copy-start.13 = (s32[1,1,1,16384]{3,2,1,0:T(1,128)S(1)}, s32[1,1,1,16384]{3,2,1,0:T(1,128)}, u32[]{:S(2)}) copy-start(s32[1,1,1,16384]{3,2,1,0:T(1,128)} %copy-done.12) | copy-start | bytes 196612
  198.8 138.9 %collective-permute-start.4 = (f32[8,24,24,4]{2,1,3,0:T(8,128)S(1)}, f32[8,24,24,4]{2,1,3,0:T(8,128)}, u32[]{:S(2)}, u32[]{:S(2)}) collective-permute-start(f32[8,24,24,4]{2,1,3,0:T(8,128)S(1)} %copy.53), channel_id=1, source_target_pairs={{1,0},{0,1},{3,2},{2,3},{5,4},{4,5},{7,6},{6,7},{9,8},{8,9},{11,10... | collective-permute-start | bytes 221192 | tf_op jit(solution)/shard_map/ppermute | solution.py:18
  202.5 138.8 %collective-permute-start.5 = (f32[8,24,24,4]{2,1,3,0:T(8,128)}, f32[8,24,24,4]{2,1,3,0:T(8,128)}, u32[]{:S(2)}, u32[]{:S(2)}) collective-permute-start(f32[8,24,24,4]{2,1,3,0:T(8,128)} %copy.55), channel_id=1, source_target_pairs={{0,1},{1,0},{2,3},{3,2},{4,5},{5,4},{6,7},{7,6},{8,9},{9,8},{10,11... | collective-permute-start | bytes 221192 | tf_op jit(solution)/shard_map/ppermute | solution.py:15
  337.7 7.3 %copy-start.9 = (f32[16,16,128]{2,1,0:T(8,128)S(1)}, f32[16,16,128]{2,1,0:T(8,128)}, u32[]{:S(2)}) copy-start(f32[16,16,128]{2,1,0:T(8,128)} %param.10) | copy-start | bytes 393220
  345.0 16.3 %copy-start.1 = (bf16[64,16,16,128]{3,2,1,0:T(8,128)(2,1)S(1)}, bf16[64,16,16,128]{3,2,1,0:T(8,128)(2,1)}, u32[]{:S(2)}) copy-start(bf16[64,16,16,128]{3,2,1,0:T(8,128)(2,1)} %param.11) | copy-start | bytes 12582916
  360.3 1.0 copy-start.4
where the time goes:
time: 426 us; the launch traced here: 422 us
  other arithmetic  141 us (33%)
  local copies, waits for them, and re-layouts  135 us (32%)
  matrix products  77.4 us (18%)
  blocking collectives  38.9 us (9%)
  starting transfers between devices  21.4 us (5%)
  waiting for transfers between devices  7.92 us (2%)
    scatter-add x1, other arithmetic, spread_terms(): jnp.zeros((orbit_count, cell_count), jnp.float32).at[:, cell_index]  94.5 us
    gather x1, local copies, waits for them, and re-layouts, gather_slots(): values = jnp.take(flat_orbitals, cell_index, axis=1)  60.6 us
    psum x1, blocking collectives, on_device(): lax.psum((gram_local, correlation_local), ('gx', 'gy', 'gz'))  38.9 us
    dot_general x1, matrix products, gather_slots(): lax.dot_general(onehot, products, (((1,), (1,)), ((), ())), precision=lax...  36.5 us
    dot_general x1, matrix products, spread_terms(): lax.dot_general(returned, onehot, (((0,), (0,)), ((), ())), precision=lax...  23.8 us
    unnamed x42, local copies, waits for them, and re-layouts  21.9 us
    add x1, other arithmetic, on_device(): local_part + nonlocal_part.reshape(orbit_count, span_one, span_two, span_...  15.3 us
    select_n x1, other arithmetic, gather_slots(): values = jnp.take(flat_orbitals, cell_index, axis=1)  13.2 us
  transfers between devices with their start and end apart: 18, of which 4 were waited for; matrix products, arithmetic and copies ran while one was open for 41% of the time, Pallas kernels for 0%

commit v1 on v0

v1 whole, which is shorter than its diff:
```python
import functools

import jax
import jax.numpy as jnp
from jax import lax
from jax.experimental import pallas as pl
from jax.experimental.pallas import tpu as pltpu
from jax.sharding import PartitionSpec as P

STENCIL_WEIGHTS = (-205.0 / 72.0, 8.0 / 5.0, -1.0 / 5.0, 8.0 / 315.0, -1.0 / 560.0)
F32, BF16 = jnp.float32, jnp.bfloat16
NT = (((1,), (1,)), ((), ()))
VMEM = pl.BlockSpec(memory_space=pltpu.VMEM)
MIB = 1024 * 1024
COLLECT_TILE = 4096
SPREAD_TILE = 4096
COLLECT_SUB = 1024
SPREAD_SUB = 1024
FLAT = ("gx", "gy")


def params(mebibytes=36):
    return pltpu.CompilerParams(vmem_limit_bytes=mebibytes * MIB)


def shifted(block, axis, step):
    count = lax.axis_size(axis)
    return lax.ppermute(block, axis, [(i, (i + step) % count) for i in range(count)])


def split_pieces(values):
    upper = values.astype(BF16).astype(F32)
    return upper, values - upper


def turn_kernel(orb_ref, rows_ref, table_ref, ends_ref, low_ref, high_ref, left_ref, right_ref):
    span_one, span_two, orbits, lanes = rows_ref.shape
    count = span_one * span_two
    half = count // 2
    lane = lax.broadcasted_iota(jnp.int32, (orbits, lanes), 1)
    packed = [None] * span_one
    for pair in range(half // 2):
        for side in range(2):
            found = []
            for r in (side * half + 2 * pair, side * half + 2 * pair + 1):
                value = orb_ref[pl.ds(r, orbits, stride=count), :]
                i, j = divmod(r, span_two)
                rows_ref[i, j] = value
                if i < 4:
                    low_ref[i, j] = value
                if i >= span_one - 4:
                    high_ref[i + 4 - span_one, j] = value
                if j < 4:
                    left_ref[i, j] = value
                if j >= span_two - 4:
                    right_ref[i, j + 4 - span_two] = value
                found.append(value)
                turned = pltpu.roll(value, (4 + 8 * j) % lanes, 1)
                packed[i] = turned if j == 0 else jnp.where(lane >= 8 * j, turned, packed[i])
                if j == span_two - 1:
                    ends_ref[i] = packed[i]
            upper, lower = split_pieces(jnp.concatenate(found, axis=0))
            low, high = pair * 2 * orbits, (pair + 1) * 2 * orbits
            for piece, base in ((upper, 0), (lower, 256)):
                base = base + side * 128
                table_ref[low:high, base : base + 128] = piece.astype(BF16)


def turn(orbitals):
    orbits, span_one, span_two, lanes = orbitals.shape
    count = span_one * span_two
    return pl.pallas_call(
        turn_kernel,
        out_shape=(
            jax.ShapeDtypeStruct((span_one, span_two, orbits, lanes), F32),
            jax.ShapeDtypeStruct((count // 2 * orbits, 512), BF16),
            jax.ShapeDtypeStruct((span_one, orbits, lanes), F32),
            jax.ShapeDtypeStruct((4, span_two, orbits, lanes), F32),
            jax.ShapeDtypeStruct((4, span_two, orbits, lanes), F32),
            jax.ShapeDtypeStruct((span_one, 4, orbits, lanes), F32),
            jax.ShapeDtypeStruct((span_one, 4, orbits, lanes), F32),
        ),
        in_specs=[VMEM],
        out_specs=(VMEM,) * 7,
        compiler_params=params(),
        cost_estimate=pl.CostEstimate(flops=2**26, bytes_accessed=2**23, transcendentals=0),
        name="turn",
    )(orbitals.reshape(orbits * count, lanes))


def cut(value, count):
    assert count & (count - 1) == 0
    return lax.shift_right_logical(value, jnp.int32(count.bit_length() - 1)), value & (count - 1)


def cell_parts(code, cells, half):
    row, lane = cut(code & (cells - 1), 128)
    group, row = cut(row, half)
    return group, row, lane


def label_parts(code, cells, atom_slots, classes):
    owner, atom = cut(cut(code, cells)[0], atom_slots)
    across = lax.shift_right_logical(owner * 43, jnp.int32(7))
    along = owner - 3 * across
    if classes == 1:
        along = jnp.zeros_like(along)
    elif classes == 2:
        along = jnp.where(along == 1, 0, 1)
    return along * 9 + across, atom


def pair_onehot(outer, outer_count, inner, inner_count, padded=0):
    tile = outer.shape[1]
    rows = lax.broadcasted_iota(jnp.int32, (inner_count, tile), 0)
    block = jnp.where(rows == inner, 1.0, 0.0)
    wide = jnp.broadcast_to(outer, (inner_count, tile))
    parts = [jnp.where(wide == at, block, 0.0) for at in range(outer_count)]
    if padded > outer_count * inner_count:
        parts.append(jnp.zeros((padded - outer_count * inner_count, tile), F32))
    return jnp.concatenate(parts, axis=0).astype(BF16)


def collect_kernel(table_ref, code_ref, profile_ref, *refs, classes, atom_slots):
    out_refs, picked_refs, total = refs[:classes], refs[classes : classes + 2], refs[-1]
    step = pl.program_id(0)
    orbits = 8
    half = table_ref.shape[0] // orbits
    cells = half * 2 * 128
    channels = profile_ref.shape[0]
    subs = COLLECT_TILE // COLLECT_SUB

    def pick(at, target):
        group, _, lane = cell_parts(code_ref[:, pl.ds(pl.multiple_of(at, COLLECT_SUB), COLLECT_SUB)], cells, half)
        spot = pair_onehot(group, 2, lane, 128)
        target[...] = jnp.dot(
            table_ref[...], jnp.concatenate([spot, spot], axis=0), preferred_element_type=F32
        )

    def add(at, picked, live=None):
        here = pl.ds(pl.multiple_of(at, COLLECT_SUB), COLLECT_SUB)
        code = code_ref[:, here]
        wide_row = jnp.broadcast_to(cell_parts(code, cells, half)[1], (orbits, COLLECT_SUB))
        if live is not None:
            wide_row = jnp.where(live, wide_row, half)
        values = jnp.zeros((orbits, COLLECT_SUB), F32)
        for r in range(half):
            values = jnp.where(wide_row == r, picked[r * orbits : (r + 1) * orbits, :], values)
        products = jnp.concatenate(
            [profile_ref[p, :, here] * values for p in range(channels)], axis=0
        )
        pieces = jnp.concatenate(split_pieces(products), axis=0).astype(BF16)
        outer, inner = label_parts(code, cells, atom_slots, classes)
        onehot = pair_onehot(outer, 9 * classes, inner, atom_slots)
        return lax.dot_general(onehot, pieces, NT, preferred_element_type=F32)

    @pl.when(step == 0)
    def _():
        total[...] = jnp.zeros_like(total)

    start = step * COLLECT_TILE
    part = None
    for s in range(subs):
        pick(start + s * COLLECT_SUB, picked_refs[s % 2])
        if s == 0:
            part = add(jnp.maximum(start - COLLECT_SUB, 0), picked_refs[1], step > 0)
        else:
            part = part + add(start + (s - 1) * COLLECT_SUB, picked_refs[(s - 1) % 2])
    total[...] += part

    @pl.when(step == pl.num_programs(0) - 1)
    def _():
        total[...] += add(start + (subs - 1) * COLLECT_SUB, picked_refs[(subs - 1) % 2])
        rows, width = out_refs[0].shape
        for c, out_ref in enumerate(out_refs):
            block = total[c * rows : (c + 1) * rows]
            out_ref[...] = block[:, :width] + block[:, width:]


def collect(table, code, profile, classes, atom_slots):
    points = code.shape[1]
    channels = profile.shape[0]
    rows, width = 9 * atom_slots, channels * 8
    return pl.pallas_call(
        functools.partial(collect_kernel, classes=classes, atom_slots=atom_slots),
        grid=(points // COLLECT_TILE,),
        out_shape=(jax.ShapeDtypeStruct((rows, width), F32),) * classes,
        in_specs=[VMEM] * 3,
        out_specs=(VMEM,) * classes,
        scratch_shapes=[
            pltpu.VMEM((table.shape[0], COLLECT_SUB), F32),
            pltpu.VMEM((table.shape[0], COLLECT_SUB), F32),
            pltpu.VMEM((rows * classes, 2 * width), F32),
        ],
        compiler_params=params(),
        cost_estimate=pl.CostEstimate(
            flops=2 * points * table.shape[0] * 512, bytes_accessed=2**21, transcendentals=0
        ),
        name="collect",
    )(table, code, profile)


def fold_kernel(*refs, rows):
    total = None
    for ref in refs[:-1]:
        for at in range(ref.shape[0] // rows):
            block = ref[at * rows : (at + 1) * rows]
            total = block if total is None else total + block
    for at in range(refs[-1].shape[0] // rows):
        refs[-1][at * rows : (at + 1) * rows] = total


def fold(stacks, rows, copies):
    return pl.pallas_call(
        functools.partial(fold_kernel, rows=rows),
        out_shape=jax.ShapeDtypeStruct((rows * copies, stacks[0].shape[1]), F32),
        in_specs=[VMEM] * len(stacks),
        out_specs=VMEM,
        compiler_params=params(),
        name="fold",
    )(*stacks)


def summed(shares):
    if len(shares) == 1:
        return (lax.psum(shares[0], ("gx", "gy", "gz")),)
    mine, other = shares
    rows = mine.shape[0]
    copies = fold((mine, shifted(other, "gz", 1)), rows, lax.axis_size(FLAT))
    mine = fold((lax.all_to_all(copies, FLAT, 0, 0, tiled=True),), rows, 1)
    return mine, shifted(mine, "gz", 1)


def merge_kernel(*refs, addends):
    total = refs[0][...]
    for ref in refs[1:addends]:
        total = total + ref[...]
    out_refs = refs[addends:]
    rows = out_refs[0].shape[0]
    for at, out_ref in enumerate(out_refs):
        out_ref[...] = total[at * rows : (at + 1) * rows]


def merge(addends, pieces):
    rows, width = addends[0].shape
    return pl.pallas_call(
        functools.partial(merge_kernel, addends=len(addends)),
        out_shape=(jax.ShapeDtypeStruct((rows // pieces, width), F32),) * pieces,
        in_specs=[VMEM] * len(addends),
        out_specs=(VMEM,) * pieces,
        compiler_params=params(),
        name="merge",
    )(*addends)


def weigh_kernel(one_ref, two_ref, three_ref, strength_ref, out_ref):
    out_ref[...] = (one_ref[...] + two_ref[...] + three_ref[...]) * strength_ref[...]


def weigh(one, two, three, strength):
    return pl.pallas_call(
        weigh_kernel,
        out_shape=jax.ShapeDtypeStruct(strength.shape, F32),
        in_specs=[VMEM] * 4,
        out_specs=VMEM,
        compiler_params=params(),
        name="weigh",
    )(one, two, three, strength)


def stack_kernel(*refs):
    rows = refs[0].shape[0]
    for at, ref in enumerate(refs[:-1]):
        refs[-1][at * rows : (at + 1) * rows] = ref[...]


def stack(blocks):
    rows, width = blocks[0].shape
    return pl.pallas_call(
        stack_kernel,
        out_shape=jax.ShapeDtypeStruct((rows * len(blocks), width), F32),
        in_specs=[VMEM] * len(blocks),
        out_specs=VMEM,
        compiler_params=params(),
        name="stack",
    )(*blocks)


def stencil_kernel(rows_ref, below_ref, above_ref, left_ref, right_ref, near_ref, far_ref, pot_ref, out_ref, tall, pair):
    span_one, span_two, orbits, lanes = rows_ref.shape
    rows = span_one * span_two * orbits
    weights = [-0.5 * w for w in STENCIL_WEIGHTS]
    tall[0:4] = below_ref[...]
    tall[4 : 4 + span_one] = rows_ref[...]
    tall[4 + span_one : 8 + span_one] = above_ref[...]
    source = lax.broadcasted_iota(jnp.int32, (lanes, lanes), 0)
    target = lax.broadcasted_iota(jnp.int32, (lanes, lanes), 1)
    ghost = jnp.where(source % 8 < 4, source % 8 - 4, source % 8 - 4 + lanes)

    def band(gap):
        found = jnp.zeros((lanes, lanes), F32)
        for d in range(1, 5):
            found = jnp.where(jnp.abs(gap) == d, weights[d], found)
        return split_pieces(found)

    main_upper, main_lower = band(source - target)
    ends_upper, ends_lower = band(ghost - target)
    ends = jnp.where(source < 16, ends_upper, jnp.where(source < 24, ends_lower, 0.0))
    first = jnp.concatenate([main_upper, main_upper], axis=0).astype(BF16)
    second = jnp.concatenate([main_lower, ends], axis=0).astype(BF16)
    lane = lax.broadcasted_iota(jnp.int32, (orbits, lanes), 1)

    def prepare(i, carry):
        upper, lower = split_pieces(rows_ref[i].reshape(span_two * orbits, lanes))
        base = pl.multiple_of(i * span_two * orbits, span_two * orbits)
        pair[pl.ds(base, span_two * orbits), :lanes] = lower.astype(BF16)
        pair[pl.ds(base, span_two * orbits), lanes : 2 * lanes] = upper.astype(BF16)
        upper, lower = split_pieces(jnp.where(lane % 8 < 4, near_ref[i], far_ref[i]))
        found = []
        for j in range(span_two):
            one = pltpu.roll(upper, (lanes - 8 * j) % lanes, 1)
            two = pltpu.roll(lower, (lanes + 8 - 8 * j) % lanes, 1)
            three = pltpu.roll(upper, (lanes + 16 - 8 * j) % lanes, 1)
            found.append(jnp.where(lane < 8, one, jnp.where(lane < 16, two, three)))
        pair[pl.ds(base, span_two * orbits), 2 * lanes :] = jnp.concatenate(
            found, axis=0
        ).astype(BF16)
        return carry

    lax.fori_loop(0, span_one, prepare, 0)
    along = jnp.dot(pair[:, : 2 * lanes], first, preferred_element_type=F32)
    along = along + jnp.dot(pair[:, lanes:], second, preferred_element_type=F32)
    out_ref[...] = along.reshape(out_ref.shape)

    def plane(i, carry):
        line = [left_ref[i, j] for j in range(4)]
        line += [rows_ref[i, j] for j in range(span_two)]
        line += [right_ref[i, j] for j in range(4)]
        for j in range(span_two):
            acc = out_ref[i, j] + line[4 + j] * (3.0 * weights[0] + pot_ref[i, j : j + 1, :])
            for d in range(1, 5):
                four = tall[i + 4 + d, j] + tall[i + 4 - d, j]
                four = four + (line[4 + j + d] + line[4 + j - d])
                acc = acc + weights[d] * four
            out_ref[i, j] = acc
        return carry

    lax.fori_loop(0, span_one, plane, 0)


def stencil(rows, below, above, left, right, near, far, potential):
    span_one, span_two, orbits, lanes = rows.shape
    return pl.pallas_call(
        stencil_kernel,
        out_shape=jax.ShapeDtypeStruct(rows.shape, F32),
        in_specs=[VMEM] * 8,
        out_specs=VMEM,
        scratch_shapes=[
            pltpu.VMEM((span_one + 8, span_two, orbits, lanes), F32),
            pltpu.VMEM((span_one * span_two * orbits, 3 * lanes), BF16),
        ],
        compiler_params=params(),
        cost_estimate=pl.CostEstimate(flops=2**24, bytes_accessed=2**22, transcendentals=0),
        name="stencil",
    )(rows, below, above, left, right, near, far, potential)


def spread_kernel(*refs, classes, atom_slots):
    back_refs = refs[:classes]
    code_ref, profile_ref, local_ref, locked_ref, gram_ref = refs[classes : classes + 5]
    out_ref, *sums_refs = refs[classes + 5 : -5]
    turned, weights_a, weights_b, total, corr_ref = refs[-5:]
    step = pl.program_id(0)
    orbits = 8
    half = total.shape[0] // orbits
    groups = total.shape[1] // 128
    cells = half * groups * 128
    locked_count = gram_ref.shape[0]
    channels = profile_ref.shape[0]
    width = back_refs[0].shape[1]
    weights = (weights_a, weights_b)
    subs = SPREAD_TILE // SPREAD_SUB

    @pl.when(step == 0)
    def _():
        whole = jnp.concatenate([ref[...] for ref in back_refs], axis=0)
        pad = turned.shape[1] - whole.shape[0]
        whole = jnp.concatenate([whole, jnp.zeros((pad, width), F32)], axis=0)
        whole = jnp.concatenate([whole, jnp.zeros((whole.shape[0], 128 - width), F32)], axis=1)
        flipped = whole.T[:width]
        turned[...] = jnp.concatenate(split_pieces(flipped), axis=0).astype(BF16)
        total[...] = jnp.zeros_like(total)

    def weigh_points(at, target):
        here = pl.ds(at, SPREAD_SUB)
        code = code_ref[:, here]
        outer, inner = label_parts(code, cells, atom_slots, classes)
        onehot = pair_onehot(outer, 9 * classes, inner, atom_slots, turned.shape[1])
        picked = jnp.dot(turned[...], onehot, preferred_element_type=F32)
        spread = jnp.zeros((orbits, SPREAD_SUB), F32)
        for p in range(channels):
            low, high = p * orbits, width + p * orbits
            term = picked[low : low + orbits] + picked[high : high + orbits]
            spread = spread + profile_ref[p, :, here] * term
        upper, lower = split_pieces(spread)
        wide_row = jnp.broadcast_to(cell_parts(code, cells, half)[1], (orbits, SPREAD_SUB))
        for pair in range(half // 2):
            first, second = wide_row == 2 * pair, wide_row == 2 * pair + 1
            for place, piece in enumerate((upper, lower)):
                both = jnp.concatenate(
                    [jnp.where(first, piece, 0.0), jnp.where(second, piece, 0.0)], axis=0
                )
                target[pair * 16 : (pair + 1) * 16, place * SPREAD_SUB : (place + 1) * SPREAD_SUB] = both.astype(BF16)

    def scatter(at, source):
        group, _, lane = cell_parts(code_ref[:, pl.ds(at, SPREAD_SUB)], cells, half)
        spot = pair_onehot(group, groups, lane, 128)
        return lax.dot_general(
            source[...], jnp.concatenate([spot, spot], axis=1), NT, preferred_element_type=F32
        )

    part = None
    for s in range(subs + 1):
        at = step * SPREAD_TILE + s * SPREAD_SUB
        if s < subs:
            weigh_points(pl.multiple_of(at, SPREAD_SUB), weights[s % 2])
        if s > 0:
            term = scatter(pl.multiple_of(at - SPREAD_SUB, SPREAD_SUB), weights[(s - 1) % 2])
            part = term if part is None else part + term
    total[...] += part

    @pl.when(step == pl.num_programs(0) - 1)
    def _():
        rows = half * orbits
        for g in range(groups):
            there = slice(g * rows, (g + 1) * rows)
            out_ref[there] = total[:, g * 128 : (g + 1) * 128] + local_ref[there]
        corr_ref[...] = jnp.zeros_like(corr_ref)
        chunk = 32

        def add(c, carry):
            base = pl.multiple_of(c * chunk * orbits, 128)
            strip = out_ref[pl.ds(base, chunk * orbits), :]
            strip = jnp.concatenate(
                [strip[m * orbits : (m + 1) * orbits] for m in range(chunk)], axis=1
            ).astype(BF16)
            held = locked_ref[:, pl.ds(pl.multiple_of(c * chunk * 128, 128), chunk * 128)]
            corr_ref[...] += lax.dot_general(strip, held, NT, preferred_element_type=F32)
            return carry

        lax.fori_loop(0, groups * half // chunk, add, 0)
        side = locked_count // 2
        corr, gram = corr_ref[...], gram_ref[...]
        rest = jnp.zeros((side - 2 * orbits, side), F32)
        sums = jnp.concatenate(
            [
                gram[:side, :side],
                gram[side:, :side],
                gram[side:, side:],
                jnp.concatenate([corr[:, :side], corr[:, side:], rest], axis=0),
            ],
            axis=1,
        )
        if len(sums_refs) == 1:
            sums_refs[0][...] = sums
        else:
            middle = sums.shape[0] // 2
            first = lax.axis_index("gz") == 0
            sums_refs[0][...] = jnp.where(first, sums[:middle], sums[middle:])
            sums_refs[1][...] = jnp.where(first, sums[middle:], sums[:middle])


def spread(backs, code, profile, local, locked_flat, gram, atom_slots):
    classes = len(backs)
    points = code.shape[1]
    channels = profile.shape[0]
    labels = 9 * classes * atom_slots
    padded = (labels + 127) // 128 * 128
    rows = local.shape[0] // 4
    locked_count = gram.shape[0]
    shares = 2 if classes == 2 else 1
    sums = jax.ShapeDtypeStruct((locked_count // 2 // shares, 2 * locked_count), F32)
    return pl.pallas_call(
        functools.partial(spread_kernel, classes=classes, atom_slots=atom_slots),
        grid=(points // SPREAD_TILE,),
        out_shape=(jax.ShapeDtypeStruct(local.shape, F32),) + (sums,) * shares,
        in_specs=[VMEM] * (classes + 5),
        out_specs=(VMEM,) * (1 + shares),
        scratch_shapes=[
            pltpu.VMEM((2 * channels * 8, padded), BF16),
            pltpu.VMEM((rows, 2 * SPREAD_SUB), BF16),
            pltpu.VMEM((rows, 2 * SPREAD_SUB), BF16),
            pltpu.VMEM((rows, 512), F32),
            pltpu.VMEM((8, locked_count), F32),
        ],
        compiler_params=params(),
        cost_estimate=pl.CostEstimate(
            flops=2 * points * rows * 1024, bytes_accessed=2**23, transcendentals=0
        ),
        name="spread",
    )(*backs, code, profile, local, locked_flat, gram)


def solve_gram(gram):
    size = gram.shape[0]
    wide = (8, 2 * size)
    rows = lax.broadcasted_iota(jnp.int32, (size, size), 0)
    lanes = lax.broadcasted_iota(jnp.int32, (size, size), 1)
    both = jnp.concatenate([jnp.where(rows == lanes, 1.0, 0.0), gram], axis=1)
    blocks = [both[8 * b : 8 * b + 8] for b in range(size // 8)]
    place = lax.broadcasted_iota(jnp.int32, wide, 0)
    scaled = []
    for k in range(0, size, 2):
        b, s = divmod(k, 8)
        last = s + 2 == 8
        one = {
            c: jnp.broadcast_to(blocks[c][:, size + k : size + k + 1], wide)
            for c in range(b, size // 8)
        }
        two = {
            c: jnp.broadcast_to(blocks[c][:, size + k + 1 : size + k + 2], wide)
            for c in range(b, size // 8)
        }
        corner, side, end = one[b][s : s + 1], two[b][s : s + 1], two[b][s + 1 : s + 2]
        first, second = blocks[b][s : s + 1], blocks[b][s + 1 : s + 2]
        factor = 1.0 / (corner * end - side * side)
        upper = (end * first - side * second) * factor
        lower = (corner * second - side * first) * factor
        if s == 0:
            scaled.append(jnp.broadcast_to(upper, wide))
        else:
            scaled[b] = jnp.where(place == s, upper, scaled[b])
        scaled[b] = jnp.where(place == s + 1, lower, scaled[b])
        for c in range(b + 1 if last else b, size // 8):
            amount = one[c] * upper + two[c] * lower
            if c == b:
                amount = jnp.where(place > s + 1, amount, 0.0)
            blocks[c] = blocks[c] - amount
    return jnp.concatenate(blocks, axis=0), jnp.concatenate(scaled, axis=0)


def finish_kernel(applied_ref, locked_ref, *refs):
    *sums_refs, out_ref, lines, sent = refs
    orbits, locked_count = out_ref.shape[0], locked_ref.shape[0]
    parts = sent.shape[0]
    block = out_ref.shape[1] // parts
    sums = sums_refs[0][...]
    if len(sums_refs) == 2:
        first = lax.axis_index("gz") == 0
        other = sums_refs[1][...]
        sums = jnp.concatenate(
            [jnp.where(first, sums, other), jnp.where(first, other, sums)], axis=0
        )
    side = locked_count // 2
    across = sums[:, side : 2 * side]
    corr = sums[:, 3 * side :]
    corr = jnp.concatenate([corr[:orbits], corr[orbits : 2 * orbits]], axis=1)
    gram = jnp.concatenate(
        [
            jnp.concatenate([sums[:, :side], across.T], axis=1),
            jnp.concatenate([across, sums[:, 2 * side : 3 * side]], axis=1),
        ],
        axis=0,
    )
    upper, scaled = solve_gram(gram)
    middle = lax.dot_general(
        corr,
        scaled[:, :locked_count],
        NT,
        precision=lax.Precision.HIGHEST,
        preferred_element_type=F32,
    )
    mixing = jnp.dot(
        middle,
        upper[:, :locked_count],
        precision=lax.Precision.HIGHEST,
        preferred_element_type=F32,
    ).astype(BF16)

    copies = []
    for part in range(parts):
        cells = slice(part * block * 128, (part + 1) * block * 128)
        amount = jnp.dot(mixing, locked_ref[:, cells], preferred_element_type=F32)
        for r in range(block):
            row = part * block + r
            lines[part, pl.ds(r, orbits, stride=block), :] = (
                applied_ref[row * orbits : (row + 1) * orbits, :] - amount[:, r * 128 : (r + 1) * 128]
            )
        for n in range(orbits):
            copy = pltpu.make_async_copy(
                lines.at[part, pl.ds(n * block, block)],
                out_ref.at[n, pl.ds(part * block, block)],
                sent.at[part, n],
            )
            copy.start()
            copies.append(copy)
    for copy in copies:
        copy.wait()


def finish(applied, locked_flat, sums, orbits):
    count = applied.shape[0] // orbits
    parts = 4
    return pl.pallas_call(
        finish_kernel,
        out_shape=jax.ShapeDtypeStruct((orbits, count, 128), F32),
        in_specs=[VMEM] * (2 + len(sums)),
        out_specs=pl.BlockSpec(memory_space=pl.ANY),
        scratch_shapes=[
            pltpu.VMEM((parts, count // parts * orbits, 128), F32),
            pltpu.SemaphoreType.DMA((parts, orbits)),
        ],
        compiler_params=params(),
        name="finish",
    )(applied, locked_flat, *sums)


def gram_kernel(locked_ref, flat_ref, gram_ref, wide):
    locked_count, span, lanes = locked_ref.shape
    chunk = 16
    pitch = 3 * chunk + 1
    for c in range(span // chunk):
        for k in range(locked_count):
            value = locked_ref[k, c * chunk : (c + 1) * chunk].astype(F32)
            for g in range(chunk // 8):
                wide[pl.ds(k * pitch + 24 * g, 8, stride=3), :] = value[8 * g : 8 * g + 8]
        for j in range(chunk):
            line = wide[pl.ds(3 * j, locked_count, stride=pitch), :]
            at = c * chunk + j
            flat_ref[:, at * lanes : (at + 1) * lanes] = line.astype(BF16)
    strip = flat_ref[...]
    part = lax.dot_general(strip, strip, NT, preferred_element_type=F32)

    @pl.when(pl.program_id(0) == 0)
    def _():
        gram_ref[...] = part

    @pl.when(pl.program_id(0) > 0)
    def _():
        gram_ref[...] += part


def gram_of(locked):
    locked_count, span_one, span_two, lanes = locked.shape
    count = span_one * span_two
    block = 64
    return pl.pallas_call(
        gram_kernel,
        grid=(count // block,),
        out_shape=(
            jax.ShapeDtypeStruct((locked_count, count * lanes), BF16),
            jax.ShapeDtypeStruct((locked_count, locked_count), F32),
        ),
        in_specs=[pl.BlockSpec((locked_count, block, lanes), lambda t: (0, t, 0))],
        out_specs=(
            pl.BlockSpec((locked_count, block * lanes), lambda t: (0, t)),
            pl.BlockSpec((locked_count, locked_count), lambda t: (0, 0)),
        ),
        scratch_shapes=[pltpu.VMEM((locked_count * 49, lanes), F32)],
        compiler_params=params(),
        cost_estimate=pl.CostEstimate(flops=2**28, bytes_accessed=2**23, transcendentals=0),
        name="gram",
    )(locked.reshape(locked_count, count, lanes))


def on_device(
    orbitals,
    potential,
    locked,
    sphere_cell,
    sphere_owner,
    sphere_atom,
    sphere_profile,
    atom_strength,
    atom_channels,
):
    orbits, span_one, span_two, span_three = orbitals.shape
    locked_count = locked.shape[0]
    atom_slots = atom_channels.shape[3]
    channels, points = sphere_profile.shape[3:]
    classes = min(lax.axis_size("gz"), 3)
    cell, owner, atom = (x.reshape(1, points) for x in (sphere_cell, sphere_owner, sphere_atom))
    cells = span_one * span_two * span_three
    code = (owner * atom_slots + atom) * cells + cell
    profile = sphere_profile.reshape(channels, 1, points)

    rows, table, ends, low, high, left, right = turn(orbitals)
    below = shifted(high, "gx", 1)
    above = shifted(low, "gx", -1)
    before = shifted(right, "gy", 1)
    after = shifted(left, "gy", -1)
    near = shifted(ends, "gz", 1)
    far = near if classes <= 2 else shifted(ends, "gz", -1)

    slots = collect(table, code, profile, classes, atom_slots)
    slots, halos = lax.optimization_barrier((slots, (below, above, before, after, near, far)))
    below, above, before, after, near, far = halos

    if classes == 1:
        parts = merge(slots, 3)
    elif classes == 2:
        parts = merge((slots[0], shifted(slots[1], "gz", 1)), 3)
    else:
        parts = merge((slots[1], shifted(slots[2], "gz", 1), shifted(slots[0], "gz", -1)), 3)
    parts = merge((parts[1], shifted(parts[2], "gx", 1), shifted(parts[0], "gx", -1)), 3)
    active = (
        jnp.arange(channels, dtype=jnp.int32)[None, :]
        < atom_channels.reshape(atom_slots)[:, None]
    )
    strength = jnp.where(active, atom_strength.reshape(atom_slots, channels), 0.0)
    strength = jnp.repeat(strength, orbits, axis=1)
    back = weigh(parts[1], shifted(parts[2], "gy", 1), shifted(parts[0], "gy", -1), strength)

    locked, back = lax.optimization_barrier((locked, back))
    flats = gram_of(locked)
    sides = shifted(back, "gy", 1), shifted(back, "gy", -1)
    sides, (locked_flat, gram) = lax.optimization_barrier((sides, flats))
    back = stack((sides[0], back, sides[1]))
    back, rows = lax.optimization_barrier((back, rows))
    local = stencil(rows, below, above, before, after, near, far, potential)
    sides = shifted(back, "gx", 1), shifted(back, "gx", -1)
    sides, local = lax.optimization_barrier((sides, local))
    back = stack((sides[0], back, sides[1]))
    backs = (back,)
    if classes == 2:
        backs = (back, shifted(back, "gz", 1))
    elif classes == 3:
        backs = (shifted(back, "gz", 1), back, shifted(back, "gz", -1))
    applied, *shares = spread(
        backs, code, profile, local.reshape(-1, span_three), locked_flat, gram, atom_slots
    )
    return finish(applied, locked_flat, summed(shares), orbits).reshape(orbitals.shape)


def solution(mesh):
    placed = (
        P(None, "gx", "gy", "gz"),
        P("gx", "gy", "gz"),
        P(None, "gx", "gy", "gz"),
        P("gx", "gy", "gz", None),
        P("gx", "gy", "gz", None),
        P("gx", "gy", "gz", None),
        P("gx", "gy", "gz", None, None),
        P("gx", "gy", "gz", None, None),
        P("gx", "gy", "gz", None),
    )
    return jax.shard_map(
        on_device, mesh=mesh, in_specs=placed, out_specs=P(None, "gx", "gy", "gz"), check_vma=False
    )
```

time: 426 us -> 115 us (0.27)
  other arithmetic: 141 us -> 1.02 us
  local copies, waits for them, and re-layouts: 135 us -> 4.56 us
  matrix products: 77.4 us -> 0 us
  Pallas kernels: 0 us -> 61.9 us
  blocking collectives: 38.9 us -> 14.4 us
    scatter-add x1 -> x0, other arithmetic: 94.5 us -> none  [spread_terms(): jnp.zeros((orbit_count, cell_count), jnp.float32).at[:, cell_index]]
    dot_general x5 -> x0, matrix products: 77.1 us -> none  [the longest x1 36.5 us: gather_slots(): lax.dot_general(onehot, products, (((1,), (1,)), ((), ())), precision=lax...]
    pallas_call x0 -> x13, Pallas kernels: none -> 61.9 us  [the longest x1 24.6 us: spread(): pl.pallas_call(functools.partial(spread_kernel, classes=classes, atom_slo...]
    gather x1 -> x0, local copies, waits for them, and re-layouts: 60.6 us -> none  [gather_slots(): values = jnp.take(flat_orbitals, cell_index, axis=1)]
    psum x1 -> x0, blocking collectives: 38.9 us -> none  [on_device(): lax.psum((gram_local, correlation_local), ('gx', 'gy', 'gz'))]
    unnamed x42 -> x14, local copies, waits for them, and re-layouts: 21.9 us -> 4.49 us
    slice x12 -> x0, local copies, waits for them, and re-layouts: 17 us -> none  [the longest x7 8.33 us: extended_2(): lax.slice_in_dim(block, 0, width, axis=dim)]
    add x2 -> x1, other arithmetic: 15.4 us -> 1.02 us  [on_device(): code = (owner * atom_slots + atom) * cells + cell]
  transfers between devices with their start and end apart: 18 -> 17, of which waited for: 4 -> 8; matrix products, arithmetic and copies ran while one was open for 41% -> 1% of each run, Pallas kernels for 0% -> 27%
where the time goes in v1:
time: 115 us
  Pallas kernels  61.9 us (54%)
  starting transfers between devices  21.7 us (19%)
  blocking collectives  14.4 us (13%)
  waiting for transfers between devices  10.8 us (9%)
  local copies, waits for them, and re-layouts  4.56 us (4%)
    pallas_call x1, Pallas kernels, spread(): pl.pallas_call(functools.partial(spread_kernel, classes=classes, atom_slo...  24.6 us
    pallas_call x1, Pallas kernels, collect(): pl.pallas_call(functools.partial(collect_kernel, classes=classes, atom_sl...  24.2 us
    ppermute x17, starting transfers between devices, shifted(): lax.ppermute(block, axis, [(i, (i + step) % count) for i in range(count)])  21.7 us
    all_to_all x1, blocking collectives, summed(): mine = fold((lax.all_to_all(copies, FLAT, 0, 0, tiled=True),), rows, 1)  14.4 us
    ppermute x17, waiting for transfers between devices, shifted(): lax.ppermute(block, axis, [(i, (i + step) % count) for i in range(count)])  10.8 us
    pallas_call x1, Pallas kernels, finish(): pl.pallas_call(finish_kernel, out_shape=jax.ShapeDtypeStruct((orbits, cou...  5.5 us
    unnamed x14, local copies, waits for them, and re-layouts  4.49 us
    pallas_call x1, Pallas kernels, gram_of(): pl.pallas_call(gram_kernel, grid=(count // block,), out_shape=(jax.ShapeD...  3.39 us
  transfers between devices with their start and end apart: 17, of which 8 were waited for; matrix products, arithmetic and copies ran while one was open for 1% of the time, Pallas kernels for 27%

profile of v1, /device:TPU:0, one launch (start us, length us, event | category | flops | bytes accessed | tf_op | source)
XLA Modules:
  0.0 114.6 jit_solution(3500506563977068205)
XLA Ops:
  0.0 1.2 %copy-done.1 = f32[8,16,16,128]{3,2,1,0:T(8,128)S(1)} copy-done((f32[8,16,16,128]{3,2,1,0:T(8,128)S(1)}, f32[8,16,16,128]{3,2,1,0:T(8,128)}, u32[]{:S(2)}) %copy-start.1) | copy-done | bytes 1048600
  1.2 0.8 turn.1
  2.0 0.5 collective-permute-start.4
  2.5 2.6 %collective-permute-start = (f32[4,16,8,128]{3,2,1,0:T(8,128)S(1)}, f32[4,16,8,128]{3,2,1,0:T(8,128)S(1)}, u32[]{:S(2)}, u32[]{:S(2)}) collective-permute-start(f32[4,16,8,128]{3,2,1,0:T(8,128)S(1)} %get-tuple-element.47), channel_id=1, source_target_pairs={{0,8},{8,16},{16,24},{24,0},{1,9},{9,17},{17,25},{25,1},{2,10},{10... | collective-permute-start | bytes 786440 | tf_op jit(solution)/shard_map/ppermute | solution.py:28
  5.1 1.0 collective-permute-start.1
  6.1 2.0 %collective-permute-start.2 = (f32[16,4,8,128]{3,2,1,0:T(8,128)S(1)}, f32[16,4,8,128]{3,2,1,0:T(8,128)S(1)}, u32[]{:S(2)}, u32[]{:S(2)}) collective-permute-start(f32[16,4,8,128]{3,2,1,0:T(8,128)S(1)} %get-tuple-element.49), channel_id=1, source_target_pairs={{0,2},{2,4},{4,6},{6,0},{1,3},{3,5},{5,7},{7,1},{8,10},{10,12},{12... | collective-permute-start | bytes 786440 | tf_op jit(solution)/shard_map/ppermute | solution.py:28
  8.1 2.0 %collective-permute-start.3 = (f32[16,4,8,128]{3,2,1,0:T(8,128)S(1)}, f32[16,4,8,128]{3,2,1,0:T(8,128)S(1)}, u32[]{:S(2)}, u32[]{:S(2)}) collective-permute-start(f32[16,4,8,128]{3,2,1,0:T(8,128)S(1)} %get-tuple-element.50), channel_id=1, source_target_pairs={{0,6},{2,0},{4,2},{6,4},{1,7},{3,1},{5,3},{7,5},{8,14},{10,8},{12,... | collective-permute-start | bytes 786440 | tf_op jit(solution)/shard_map/ppermute | solution.py:28
  10.1 1.0 add_bitcast_fusion.code_ref.refs_2_
  11.1 0.0 copy-start.3
  11.1 1.1 copy-done.3
  12.2 24.2 %collect.1 = (f32[288,72]{1,0:T(8,128)S(1)}, f32[288,72]{1,0:T(8,128)S(1)}) custom-call(bf16[1024,512]{1,0:T(8,128)(2,1)S(1)} %get-tuple-element.44.table_ref, s32[1,16384]{1,0:T(1,128)S(1)} %add_bitcast_fusion.code_ref.refs_2_, f32[9,1,16384]{2,1,0:T(1,128)S(1)} %bitcast.19), custom_call_target="tpu_custom_call" | custom-call | flops 17179869184 | bytes 2097152 | tf_op jit(solution)/shard_map/collect/pallas_call | solution.py:184
  36.4 0.0 copy-start.2
  36.4 0.0 collective-permute-done.4.near_ref.far_ref
  36.4 0.0 collective-permute-done.below_ref
  36.4 0.0 collective-permute-done.1.above_ref
  36.4 0.0 collective-permute-done.2.left_ref
  36.5 0.0 collective-permute-done.3.right_ref
  36.5 0.1 collective-permute-start.5
  36.5 1.4 %collective-permute-done.5.refs_1_ = f32[288,72]{1,0:T(8,128)S(1)} collective-permute-done((f32[288,72]{1,0:T(8,128)S(1)}, f32[288,72]{1,0:T(8,128)S(1)}, u32[]{:S(2)}, u32[]{:S(2)}) %collective-permute-start.5) | collective-permute-done | bytes 82976 | tf_op jit(solution)/shard_map/ppermute | solution.py:28
  37.9 0.9 collective-permute-start.6
  38.8 2.1 %collective-permute-start.7 = (f32[96,72]{1,0:T(8,128)S(1)}, f32[96,72]{1,0:T(8,128)S(1)}, u32[]{:S(2)}, u32[]{:S(2)}) collective-permute-start(f32[96,72]{1,0:T(8,128)S(1)} %get-tuple-element.56), channel_id=1, source_target_pairs={{0,24},{8,0},{16,8},{24,16},{1,25},{9,1},{17,9},{25,17},{2,26},{10... | collective-permute-start | bytes 82952 | tf_op jit(solution)/shard_map/ppermute | solution.py:28
  40.9 2.3 %collective-permute-done.6.refs_1_ = f32[96,72]{1,0:T(8,128)S(1)} collective-permute-done((f32[96,72]{1,0:T(8,128)S(1)}, f32[96,72]{1,0:T(8,128)S(1)}, u32[]{:S(2)}, u32[]{:S(2)}) %collective-permute-start.6) | collective-permute-done | bytes 27680 | tf_op jit(solution)/shard_map/ppermute | solution.py:28
  43.3 0.7 collective-permute-done.7.refs_2_
  44.0 0.1 collective-permute-start.8
  44.1 3.8 %collective-permute-start.9 = (f32[32,72]{1,0:T(8,128)S(1)}, f32[32,72]{1,0:T(8,128)S(1)}, u32[]{:S(2)}, u32[]{:S(2)}) collective-permute-start(f32[32,72]{1,0:T(8,128)S(1)} %get-tuple-element.59), channel_id=1, source_target_pairs={{0,6},{2,0},{4,2},{6,4},{1,7},{3,1},{5,3},{7,5},{8,14},{10,8},{12,... | collective-permute-start | bytes 27656 | tf_op jit(solution)/shard_map/ppermute | solution.py:28
  47.9 0.1 copy.11.strength_ref
  48.0 1.6 %collective-permute-done.8.two_ref = f32[32,72]{1,0:T(8,128)S(1)} collective-permute-done((f32[32,72]{1,0:T(8,128)S(1)}, f32[32,72]{1,0:T(8,128)S(1)}, u32[]{:S(2)}, u32[]{:S(2)}) %collective-permute-start.8) | collective-permute-done | bytes 9248 | tf_op jit(solution)/shard_map/ppermute | solution.py:28
  49.6 0.0 collective-permute-done.9.three_ref
  49.6 3.9 %collective-permute-start.11 = (f32[32,72]{1,0:T(8,128)S(1)}, f32[32,72]{1,0:T(8,128)S(1)}, u32[]{:S(2)}, u32[]{:S(2)}) collective-permute-start(f32[32,72]{1,0:T(8,128)S(1)} %weigh.1.refs_1_), channel_id=1, source_target_pairs={{0,6},{2,0},{4,2},{6,4},{1,7},{3,1},{5,3},{7,5},{8,14},{10,8},{12,... | collective-permute-start | bytes 27656 | tf_op jit(solution)/shard_map/ppermute | solution.py:28
  53.5 0.0 collective-permute-start.10
  53.5 2.2 %copy-done = bf16[64,16,16,128]{3,2,1,0:T(8,128)(2,1)S(1)} copy-done((bf16[64,16,16,128]{3,2,1,0:T(8,128)(2,1)S(1)}, bf16[64,16,16,128]{3,2,1,0:T(8,128)(2,1)}, u32[]{:S(2)}) %copy-start) | copy-done | bytes 4194328
  55.7 3.4 %gram.1 = (bf16[64,32768]{1,0:T(8,128)(2,1)S(1)}, f32[64,64]{1,0:T(8,128)S(1)}) custom-call(bf16[64,256,128]{2,1,0:T(8,128)(2,1)S(1)} %bitcast.14), custom_call_target="tpu_custom_call" | custom-call | flops 268435456 | bytes 8388608 | tf_op jit(solution)/shard_map/gram/pallas_call | solution.py:647
  59.1 0.0 collective-permute-done.11.refs_2_
  59.1 0.0 collective-permute-done.10.refs_0_
  59.1 1.9 %collective-permute-start.13 = (f32[96,72]{1,0:T(8,128)S(1)}, f32[96,72]{1,0:T(8,128)S(1)}, u32[]{:S(2)}, u32[]{:S(2)}) collective-permute-start(f32[96,72]{1,0:T(8,128)S(1)} %stack.2.refs_1_), channel_id=1, source_target_pairs={{0,24},{8,0},{16,8},{24,16},{1,25},{9,1},{17,9},{25,17},{2,26},{10... | collective-permute-start | bytes 82952 | tf_op jit(solution)/shard_map/ppermute | solution.py:28
  61.1 0.5 collective-permute-start.12
  61.6 3.3 %stencil.1 = f32[16,16,8,128]{3,2,1,0:T(8,128)S(1)} custom-call(f32[16,16,8,128]{3,2,1,0:T(8,128)S(1)} %get-tuple-element.68.rows_ref, f32[4,16,8,128]{3,2,1,0:T(8,128)S(1)} %collective-permute-done.below_ref, f32[4,16,8,128]{3,2,1,0:T(8,128)S(1)} %collective-permute-done.1.above_ref, f32[16,4,8,128]{3,2,1,0:T(8,128)S(1)} %collective-permute-done.2.left_ref, ...), custom_call_target="tpu_custom_call" | custom-call | flops 16777216 | bytes 4194304 | tf_op jit(solution)/shard_map/stencil/pallas_call | solution.py:353
  64.9 0.0 collective-permute-done.13.refs_2_
  64.9 1.1 collective-permute-done.12.refs_0_
  66.1 0.1 collective-permute-start.14
  66.1 1.4 %collective-permute-done.14.refs_1_ = f32[288,72]{1,0:T(8,128)S(1)} collective-permute-done((f32[288,72]{1,0:T(8,128)S(1)}, f32[288,72]{1,0:T(8,128)S(1)}, u32[]{:S(2)}, u32[]{:S(2)}) %collective-permute-start.14) | collective-permute-done | bytes 82976 | tf_op jit(solution)/shard_map/ppermute | solution.py:28
  67.5 24.6 %spread.1 = (f32[2048,128]{1,0:T(8,128)S(1)}, f32[16,128]{1,0:T(8,128)S(1)}, f32[16,128]{1,0:T(8,128)S(1)}) custom-call(f32[288,72]{1,0:T(8,128)S(1)} %stack.3.refs_0_, f32[288,72]{1,0:T(8,128)S(1)} %collective-permute-done.14.refs_1_, s32[1,16384]{1,0:T(1,128)S(1)} %add_bitcast_fusion.code_ref.refs_2_, f32[9,1,16384]{2,1,0:T(1,128)S(1)} %bitcast.20, ...), custom_call_target="tpu_custom_call" | custom-call | flops 17179869184 | bytes 8388608 | tf_op jit(solution)/shard_map/spread/pallas_call | solution.py:483
  92.1 0.2 collective-permute-start.15
  92.3 1.0 collective-permute-done.15.refs_1_
  93.3 14.4 %all_to_all.11 = f32[16,16,128]{2,1,0:T(8,128)S(1)} all-to-all(f32[16,16,128]{2,1,0:T(8,128)S(1)} %bitcast.17), channel_id=1, replica_groups=mesh['gx'=4,'gy'=4,'gz'=2] {'gx','gy'}, dimensions={0} | all-to-all | bytes 262144 | tf_op jit(solution)/shard_map/all_to_all | solution.py:230
  107.7 0.1 collective-permute-start.16
  107.8 1.2 %collective-permute-done.16.refs_1_ = f32[16,128]{1,0:T(8,128)S(1)} collective-permute-done((f32[16,128]{1,0:T(8,128)S(1)}, f32[16,128]{1,0:T(8,128)S(1)}, u32[]{:S(2)}, u32[]{:S(2)}) %collective-permute-start.16) | collective-permute-done | bytes 8224 | tf_op jit(solution)/shard_map/ppermute | solution.py:28
  109.0 5.5 %finish.1 = f32[8,256,128]{2,1,0:T(8,128)} custom-call(f32[2048,128]{1,0:T(8,128)S(1)} %get-tuple-element.80.applied_ref, bf16[64,32768]{1,0:T(8,128)(2,1)S(1)} %get-tuple-element.78.refs_5_.locked_ref, f32[16,128]{1,0:T(8,128)S(1)} %fold.3.refs_0_, f32[16,128]{1,0:T(8,128)S(1)} %collective-permute-done.16.refs_1_), custom_call_target="tpu_custom_call" | custom-call | tf_op jit(solution)/shard_map/finish/pallas_call | solution.py:604
  (18 shorter events, 0.1 us)
Async XLA Ops:
  0.0 1.2 %copy-start.1 = (f32[8,16,16,128]{3,2,1,0:T(8,128)S(1)}, f32[8,16,16,128]{3,2,1,0:T(8,128)}, u32[]{:S(2)}) copy-start(f32[8,16,16,128]{3,2,1,0:T(8,128)} %param.9) | copy-start | bytes 3145732
  2.0 34.4 %collective-permute-start.4 = (f32[16,8,128]{2,1,0:T(8,128)S(1)}, f32[16,8,128]{2,1,0:T(8,128)S(1)}, u32[]{:S(2)}, u32[]{:S(2)}) collective-permute-start(f32[16,8,128]{2,1,0:T(8,128)S(1)} %get-tuple-element.51), channel_id=1, source_target_pairs={{0,1},{1,0},{2,3},{3,2},{4,5},{5,4},{6,7},{7,6},{8,9},{9,8},{10,11... | collective-permute-start | bytes 196616 | tf_op jit(solution)/shard_map/ppermute | solution.py:28
  2.5 33.9 %collective-permute-start = (f32[4,16,8,128]{3,2,1,0:T(8,128)S(1)}, f32[4,16,8,128]{3,2,1,0:T(8,128)S(1)}, u32[]{:S(2)}, u32[]{:S(2)}) collective-permute-start(f32[4,16,8,128]{3,2,1,0:T(8,128)S(1)} %get-tuple-element.47), channel_id=1, source_target_pairs={{0,8},{8,16},{16,24},{24,0},{1,9},{9,17},{17,25},{25,1},{2,10},{10... | collective-permute-start | bytes 786440 | tf_op jit(solution)/shard_map/ppermute | solution.py:28
  5.1 31.4 %collective-permute-start.1 = (f32[4,16,8,128]{3,2,1,0:T(8,128)S(1)}, f32[4,16,8,128]{3,2,1,0:T(8,128)S(1)}, u32[]{:S(2)}, u32[]{:S(2)}) collective-permute-start(f32[4,16,8,128]{3,2,1,0:T(8,128)S(1)} %get-tuple-element.48), channel_id=1, source_target_pairs={{0,24},{8,0},{16,8},{24,16},{1,25},{9,1},{17,9},{25,17},{2,26},{10... | collective-permute-start | bytes 786440 | tf_op jit(solution)/shard_map/ppermute | solution.py:28
  6.1 30.3 %collective-permute-start.2 = (f32[16,4,8,128]{3,2,1,0:T(8,128)S(1)}, f32[16,4,8,128]{3,2,1,0:T(8,128)S(1)}, u32[]{:S(2)}, u32[]{:S(2)}) collective-permute-start(f32[16,4,8,128]{3,2,1,0:T(8,128)S(1)} %get-tuple-element.49), channel_id=1, source_target_pairs={{0,2},{2,4},{4,6},{6,0},{1,3},{3,5},{5,7},{7,1},{8,10},{10,12},{12... | collective-permute-start | bytes 786440 | tf_op jit(solution)/shard_map/ppermute | solution.py:28
  8.1 28.4 %collective-permute-start.3 = (f32[16,4,8,128]{3,2,1,0:T(8,128)S(1)}, f32[16,4,8,128]{3,2,1,0:T(8,128)S(1)}, u32[]{:S(2)}, u32[]{:S(2)}) collective-permute-start(f32[16,4,8,128]{3,2,1,0:T(8,128)S(1)} %get-tuple-element.50), channel_id=1, source_target_pairs={{0,6},{2,0},{4,2},{6,4},{1,7},{3,1},{5,3},{7,5},{8,14},{10,8},{12,... | collective-permute-start | bytes 786440 | tf_op jit(solution)/shard_map/ppermute | solution.py:28
  11.1 1.1 copy-start.3
  12.2 28.7 %copy-start.5 = (f32[1,1,1,32,9]{3,2,4,1,0:T(1,128)S(1)}, f32[1,1,1,32,9]{3,2,4,1,0:T(1,128)}, u32[]{:S(2)}) copy-start(f32[1,1,1,32,9]{3,2,4,1,0:T(1,128)} %param.16) | copy-start | bytes 3460
  12.2 28.7 %copy-start.6 = (s32[1,1,1,32]{3,2,1,0:T(1,128)S(1)}, s32[1,1,1,32]{3,2,1,0:T(1,128)}, u32[]{:S(2)}) copy-start(s32[1,1,1,32]{3,2,1,0:T(1,128)} %param.17) | copy-start | bytes 388
  12.2 55.3 %copy-start.4 = (f32[1,1,1,9,16384]{4,2,3,1,0:T(1,128)S(1)}, f32[1,1,1,9,16384]{4,2,3,1,0:T(1,128)}, u32[]{:S(2)}) copy-start(f32[1,1,1,9,16384]{4,2,3,1,0:T(1,128)} %param.15) | copy-start | bytes 1769476
  36.4 25.2 %copy-start.2 = (f32[16,16,128]{2,1,0:T(8,128)S(1)}, f32[16,16,128]{2,1,0:T(8,128)}, u32[]{:S(2)}) copy-start(f32[16,16,128]{2,1,0:T(8,128)} %pot_ref.1) | copy-start | bytes 393220
  36.5 1.4 %collective-permute-start.5 = (f32[288,72]{1,0:T(8,128)S(1)}, f32[288,72]{1,0:T(8,128)S(1)}, u32[]{:S(2)}, u32[]{:S(2)}) collective-permute-start(f32[288,72]{1,0:T(8,128)S(1)} %get-tuple-element.53), channel_id=1, source_target_pairs={{0,1},{1,0},{2,3},{3,2},{4,5},{5,4},{6,7},{7,6},{8,9},{9,8},{10,11... | collective-permute-start | bytes 248840 | tf_op jit(solution)/shard_map/ppermute | solution.py:28
  37.9 5.3 %collective-permute-start.6 = (f32[96,72]{1,0:T(8,128)S(1)}, f32[96,72]{1,0:T(8,128)S(1)}, u32[]{:S(2)}, u32[]{:S(2)}) collective-permute-start(f32[96,72]{1,0:T(8,128)S(1)} %get-tuple-element.55), channel_id=1, source_target_pairs={{0,8},{8,16},{16,24},{24,0},{1,9},{9,17},{17,25},{25,1},{2,10},{10... | collective-permute-start | bytes 82952 | tf_op jit(solution)/shard_map/ppermute | solution.py:28
  38.8 5.2 %collective-permute-start.7 = (f32[96,72]{1,0:T(8,128)S(1)}, f32[96,72]{1,0:T(8,128)S(1)}, u32[]{:S(2)}, u32[]{:S(2)}) collective-permute-start(f32[96,72]{1,0:T(8,128)S(1)} %get-tuple-element.56), channel_id=1, source_target_pairs={{0,24},{8,0},{16,8},{24,16},{1,25},{9,1},{17,9},{25,17},{2,26},{10... | collective-permute-start | bytes 82952 | tf_op jit(solution)/shard_map/ppermute | solution.py:28
  44.0 5.6 %collective-permute-start.8 = (f32[32,72]{1,0:T(8,128)S(1)}, f32[32,72]{1,0:T(8,128)S(1)}, u32[]{:S(2)}, u32[]{:S(2)}) collective-permute-start(f32[32,72]{1,0:T(8,128)S(1)} %get-tuple-element.58), channel_id=1, source_target_pairs={{0,2},{2,4},{4,6},{6,0},{1,3},{3,5},{5,7},{7,1},{8,10},{10,12},{12... | collective-permute-start | bytes 27656 | tf_op jit(solution)/shard_map/ppermute | solution.py:28
  44.1 5.5 %collective-permute-start.9 = (f32[32,72]{1,0:T(8,128)S(1)}, f32[32,72]{1,0:T(8,128)S(1)}, u32[]{:S(2)}, u32[]{:S(2)}) collective-permute-start(f32[32,72]{1,0:T(8,128)S(1)} %get-tuple-element.59), channel_id=1, source_target_pairs={{0,6},{2,0},{4,2},{6,4},{1,7},{3,1},{5,3},{7,5},{8,14},{10,8},{12,... | collective-permute-start | bytes 27656 | tf_op jit(solution)/shard_map/ppermute | solution.py:28
  49.6 9.5 %collective-permute-start.11 = (f32[32,72]{1,0:T(8,128)S(1)}, f32[32,72]{1,0:T(8,128)S(1)}, u32[]{:S(2)}, u32[]{:S(2)}) collective-permute-start(f32[32,72]{1,0:T(8,128)S(1)} %weigh.1.refs_1_), channel_id=1, source_target_pairs={{0,6},{2,0},{4,2},{6,4},{1,7},{3,1},{5,3},{7,5},{8,14},{10,8},{12,... | collective-permute-start | bytes 27656 | tf_op jit(solution)/shard_map/ppermute | solution.py:28
  53.5 5.6 %collective-permute-start.10 = (f32[32,72]{1,0:T(8,128)S(1)}, f32[32,72]{1,0:T(8,128)S(1)}, u32[]{:S(2)}, u32[]{:S(2)}) collective-permute-start(f32[32,72]{1,0:T(8,128)S(1)} %weigh.1.refs_1_), channel_id=1, source_target_pairs={{0,2},{2,4},{4,6},{6,0},{1,3},{3,5},{5,7},{7,1},{8,10},{10,12},{12... | collective-permute-start | bytes 27656 | tf_op jit(solution)/shard_map/ppermute | solution.py:28
  53.5 2.2 %copy-start = (bf16[64,16,16,128]{3,2,1,0:T(8,128)(2,1)S(1)}, bf16[64,16,16,128]{3,2,1,0:T(8,128)(2,1)}, u32[]{:S(2)}) copy-start(bf16[64,16,16,128]{3,2,1,0:T(8,128)(2,1)} %param.11) | copy-start | bytes 12582916
  59.1 5.8 %collective-permute-start.13 = (f32[96,72]{1,0:T(8,128)S(1)}, f32[96,72]{1,0:T(8,128)S(1)}, u32[]{:S(2)}, u32[]{:S(2)}) collective-permute-start(f32[96,72]{1,0:T(8,128)S(1)} %stack.2.refs_1_), channel_id=1, source_target_pairs={{0,24},{8,0},{16,8},{24,16},{1,25},{9,1},{17,9},{25,17},{2,26},{10... | collective-permute-start | bytes 82952 | tf_op jit(solution)/shard_map/ppermute | solution.py:28
  61.1 5.0 %collective-permute-start.12 = (f32[96,72]{1,0:T(8,128)S(1)}, f32[96,72]{1,0:T(8,128)S(1)}, u32[]{:S(2)}, u32[]{:S(2)}) collective-permute-start(f32[96,72]{1,0:T(8,128)S(1)} %stack.2.refs_1_), channel_id=1, source_target_pairs={{0,8},{8,16},{16,24},{24,0},{1,9},{9,17},{17,25},{25,1},{2,10},{10... | collective-permute-start | bytes 82952 | tf_op jit(solution)/shard_map/ppermute | solution.py:28
  66.1 1.4 %collective-permute-start.14 = (f32[288,72]{1,0:T(8,128)S(1)}, f32[288,72]{1,0:T(8,128)S(1)}, u32[]{:S(2)}, u32[]{:S(2)}) collective-permute-start(f32[288,72]{1,0:T(8,128)S(1)} %stack.3.refs_0_), channel_id=1, source_target_pairs={{0,1},{1,0},{2,3},{3,2},{4,5},{5,4},{6,7},{7,6},{8,9},{9,8},{10,11... | collective-permute-start | bytes 248840 | tf_op jit(solution)/shard_map/ppermute | solution.py:28
  92.1 1.2 %collective-permute-start.15 = (f32[16,128]{1,0:T(8,128)S(1)}, f32[16,128]{1,0:T(8,128)S(1)}, u32[]{:S(2)}, u32[]{:S(2)}) collective-permute-start(f32[16,128]{1,0:T(8,128)S(1)} %get-tuple-element.82), channel_id=1, source_target_pairs={{0,1},{1,0},{2,3},{3,2},{4,5},{5,4},{6,7},{7,6},{8,9},{9,8},{10,11... | collective-permute-start | bytes 24584 | tf_op jit(solution)/shard_map/ppermute | solution.py:28
  107.7 1.2 %collective-permute-start.16 = (f32[16,128]{1,0:T(8,128)S(1)}, f32[16,128]{1,0:T(8,128)S(1)}, u32[]{:S(2)}, u32[]{:S(2)}) collective-permute-start(f32[16,128]{1,0:T(8,128)S(1)} %fold.3.refs_0_), channel_id=1, source_target_pairs={{0,1},{1,0},{2,3},{3,2},{4,5},{5,4},{6,7},{7,6},{8,9},{9,8},{10,11... | collective-permute-start | bytes 24584 | tf_op jit(solution)/shard_map/ppermute | solution.py:28

commit v2 on v1

--- a/solution.py
+++ b/solution.py
@@ -13,9 +13,9 @@
 VMEM = pl.BlockSpec(memory_space=pltpu.VMEM)
 MIB = 1024 * 1024
 COLLECT_TILE = 4096
-SPREAD_TILE = 4096
-COLLECT_SUB = 1024
-SPREAD_SUB = 1024
+SPREAD_TILE = 16384
+COLLECT_SUB = 512
+SPREAD_SUB = 2048
 FLAT = ("gx", "gy")
 
 

time: 115 us -> 114 us (level)
  no operation moved by 1% of the time
where the time goes in v2:
time: 114 us
  Pallas kernels  60.9 us (53%)
  starting transfers between devices  21.5 us (19%)
  blocking collectives  14.4 us (13%)
  waiting for transfers between devices  10.8 us (9%)
  local copies, waits for them, and re-layouts  4.56 us (4%)
    pallas_call x1, Pallas kernels, spread(): pl.pallas_call(functools.partial(spread_kernel, classes=classes, atom_slo...  23.9 us
    pallas_call x1, Pallas kernels, collect(): pl.pallas_call(functools.partial(collect_kernel, classes=classes, atom_sl...  23.8 us
    ppermute x17, starting transfers between devices, shifted(): lax.ppermute(block, axis, [(i, (i + step) % count) for i in range(count)])  21.5 us
    all_to_all x1, blocking collectives, summed(): mine = fold((lax.all_to_all(copies, FLAT, 0, 0, tiled=True),), rows, 1)  14.4 us
    ppermute x17, waiting for transfers between devices, shifted(): lax.ppermute(block, axis, [(i, (i + step) % count) for i in range(count)])  10.8 us
    pallas_call x1, Pallas kernels, finish(): pl.pallas_call(finish_kernel, out_shape=jax.ShapeDtypeStruct((orbits, cou...  5.5 us
    unnamed x14, local copies, waits for them, and re-layouts  4.49 us
    pallas_call x1, Pallas kernels, stencil(): pl.pallas_call(stencil_kernel, out_shape=jax.ShapeDtypeStruct(rows.shape,...  3.52 us
  transfers between devices with their start and end apart: 17, of which 8 were waited for; matrix products, arithmetic and copies ran while one was open for 1% of the time, Pallas kernels for 27%

profile of v2, /device:TPU:0, one launch (start us, length us, event | category | flops | bytes accessed | tf_op | source)
XLA Modules:
  0.0 113.6 jit_solution(3588938322849227231)
XLA Ops:
  0.0 1.2 %copy-done.1 = f32[8,16,16,128]{3,2,1,0:T(8,128)S(1)} copy-done((f32[8,16,16,128]{3,2,1,0:T(8,128)S(1)}, f32[8,16,16,128]{3,2,1,0:T(8,128)}, u32[]{:S(2)}) %copy-start.1) | copy-done | bytes 1048600
  1.2 0.8 turn.1
  2.0 0.5 collective-permute-start.4
  2.5 2.6 %collective-permute-start = (f32[4,16,8,128]{3,2,1,0:T(8,128)S(1)}, f32[4,16,8,128]{3,2,1,0:T(8,128)S(1)}, u32[]{:S(2)}, u32[]{:S(2)}) collective-permute-start(f32[4,16,8,128]{3,2,1,0:T(8,128)S(1)} %get-tuple-element.47), channel_id=1, source_target_pairs={{0,8},{8,16},{16,24},{24,0},{1,9},{9,17},{17,25},{25,1},{2,10},{10... | collective-permute-start | bytes 786440 | tf_op jit(solution)/shard_map/ppermute | solution.py:28
  5.1 1.0 collective-permute-start.1
  6.1 2.0 %collective-permute-start.2 = (f32[16,4,8,128]{3,2,1,0:T(8,128)S(1)}, f32[16,4,8,128]{3,2,1,0:T(8,128)S(1)}, u32[]{:S(2)}, u32[]{:S(2)}) collective-permute-start(f32[16,4,8,128]{3,2,1,0:T(8,128)S(1)} %get-tuple-element.49), channel_id=1, source_target_pairs={{0,2},{2,4},{4,6},{6,0},{1,3},{3,5},{5,7},{7,1},{8,10},{10,12},{12... | collective-permute-start | bytes 786440 | tf_op jit(solution)/shard_map/ppermute | solution.py:28
  8.1 2.0 %collective-permute-start.3 = (f32[16,4,8,128]{3,2,1,0:T(8,128)S(1)}, f32[16,4,8,128]{3,2,1,0:T(8,128)S(1)}, u32[]{:S(2)}, u32[]{:S(2)}) collective-permute-start(f32[16,4,8,128]{3,2,1,0:T(8,128)S(1)} %get-tuple-element.50), channel_id=1, source_target_pairs={{0,6},{2,0},{4,2},{6,4},{1,7},{3,1},{5,3},{7,5},{8,14},{10,8},{12,... | collective-permute-start | bytes 786440 | tf_op jit(solution)/shard_map/ppermute | solution.py:28
  10.1 1.0 add_bitcast_fusion.code_ref.refs_2_
  11.1 0.0 copy-start.3
  11.1 1.1 copy-done.3
  12.2 23.8 %collect.1 = (f32[288,72]{1,0:T(8,128)S(1)}, f32[288,72]{1,0:T(8,128)S(1)}) custom-call(bf16[1024,512]{1,0:T(8,128)(2,1)S(1)} %get-tuple-element.44.table_ref, s32[1,16384]{1,0:T(1,128)S(1)} %add_bitcast_fusion.code_ref.refs_2_, f32[9,1,16384]{2,1,0:T(1,128)S(1)} %bitcast.19), custom_call_target="tpu_custom_call" | custom-call | flops 17179869184 | bytes 2097152 | tf_op jit(solution)/shard_map/collect/pallas_call | solution.py:184
  36.0 0.0 copy-start.2
  36.0 0.0 collective-permute-done.4.near_ref.far_ref
  36.0 0.0 collective-permute-done.below_ref
  36.1 0.0 collective-permute-done.1.above_ref
  36.1 0.0 collective-permute-done.2.left_ref
  36.1 0.0 collective-permute-done.3.right_ref
  36.1 0.1 collective-permute-start.5
  36.2 1.4 %collective-permute-done.5.refs_1_ = f32[288,72]{1,0:T(8,128)S(1)} collective-permute-done((f32[288,72]{1,0:T(8,128)S(1)}, f32[288,72]{1,0:T(8,128)S(1)}, u32[]{:S(2)}, u32[]{:S(2)}) %collective-permute-start.5) | collective-permute-done | bytes 82976 | tf_op jit(solution)/shard_map/ppermute | solution.py:28
  37.5 0.9 collective-permute-start.6
  38.4 2.1 %collective-permute-start.7 = (f32[96,72]{1,0:T(8,128)S(1)}, f32[96,72]{1,0:T(8,128)S(1)}, u32[]{:S(2)}, u32[]{:S(2)}) collective-permute-start(f32[96,72]{1,0:T(8,128)S(1)} %get-tuple-element.56), channel_id=1, source_target_pairs={{0,24},{8,0},{16,8},{24,16},{1,25},{9,1},{17,9},{25,17},{2,26},{10... | collective-permute-start | bytes 82952 | tf_op jit(solution)/shard_map/ppermute | solution.py:28
  40.5 2.3 %collective-permute-done.6.refs_1_ = f32[96,72]{1,0:T(8,128)S(1)} collective-permute-done((f32[96,72]{1,0:T(8,128)S(1)}, f32[96,72]{1,0:T(8,128)S(1)}, u32[]{:S(2)}, u32[]{:S(2)}) %collective-permute-start.6) | collective-permute-done | bytes 27680 | tf_op jit(solution)/shard_map/ppermute | solution.py:28
  42.9 0.7 collective-permute-done.7.refs_2_
  43.6 0.1 collective-permute-start.8
  43.7 3.8 %collective-permute-start.9 = (f32[32,72]{1,0:T(8,128)S(1)}, f32[32,72]{1,0:T(8,128)S(1)}, u32[]{:S(2)}, u32[]{:S(2)}) collective-permute-start(f32[32,72]{1,0:T(8,128)S(1)} %get-tuple-element.59), channel_id=1, source_target_pairs={{0,6},{2,0},{4,2},{6,4},{1,7},{3,1},{5,3},{7,5},{8,14},{10,8},{12,... | collective-permute-start | bytes 27656 | tf_op jit(solution)/shard_map/ppermute | solution.py:28
  47.5 0.1 copy.11.strength_ref
  47.6 1.6 %collective-permute-done.8.two_ref = f32[32,72]{1,0:T(8,128)S(1)} collective-permute-done((f32[32,72]{1,0:T(8,128)S(1)}, f32[32,72]{1,0:T(8,128)S(1)}, u32[]{:S(2)}, u32[]{:S(2)}) %collective-permute-start.8) | collective-permute-done | bytes 9248 | tf_op jit(solution)/shard_map/ppermute | solution.py:28
  49.2 0.0 collective-permute-done.9.three_ref
  49.2 3.9 %collective-permute-start.11 = (f32[32,72]{1,0:T(8,128)S(1)}, f32[32,72]{1,0:T(8,128)S(1)}, u32[]{:S(2)}, u32[]{:S(2)}) collective-permute-start(f32[32,72]{1,0:T(8,128)S(1)} %weigh.1.refs_1_), channel_id=1, source_target_pairs={{0,6},{2,0},{4,2},{6,4},{1,7},{3,1},{5,3},{7,5},{8,14},{10,8},{12,... | collective-permute-start | bytes 27656 | tf_op jit(solution)/shard_map/ppermute | solution.py:28
  53.1 0.0 collective-permute-start.10
  53.1 2.2 %copy-done = bf16[64,16,16,128]{3,2,1,0:T(8,128)(2,1)S(1)} copy-done((bf16[64,16,16,128]{3,2,1,0:T(8,128)(2,1)S(1)}, bf16[64,16,16,128]{3,2,1,0:T(8,128)(2,1)}, u32[]{:S(2)}) %copy-start) | copy-done | bytes 4194328
  55.3 3.4 %gram.1 = (bf16[64,32768]{1,0:T(8,128)(2,1)S(1)}, f32[64,64]{1,0:T(8,128)S(1)}) custom-call(bf16[64,256,128]{2,1,0:T(8,128)(2,1)S(1)} %bitcast.14), custom_call_target="tpu_custom_call" | custom-call | flops 268435456 | bytes 8388608 | tf_op jit(solution)/shard_map/gram/pallas_call | solution.py:647
  58.7 0.0 collective-permute-done.11.refs_2_
  58.7 0.0 collective-permute-done.10.refs_0_
  58.7 1.9 %collective-permute-start.13 = (f32[96,72]{1,0:T(8,128)S(1)}, f32[96,72]{1,0:T(8,128)S(1)}, u32[]{:S(2)}, u32[]{:S(2)}) collective-permute-start(f32[96,72]{1,0:T(8,128)S(1)} %stack.2.refs_1_), channel_id=1, source_target_pairs={{0,24},{8,0},{16,8},{24,16},{1,25},{9,1},{17,9},{25,17},{2,26},{10... | collective-permute-start | bytes 82952 | tf_op jit(solution)/shard_map/ppermute | solution.py:28
  60.7 0.3 collective-permute-start.12
  61.0 3.5 %stencil.1 = f32[16,16,8,128]{3,2,1,0:T(8,128)S(1)} custom-call(f32[16,16,8,128]{3,2,1,0:T(8,128)S(1)} %get-tuple-element.68.rows_ref, f32[4,16,8,128]{3,2,1,0:T(8,128)S(1)} %collective-permute-done.below_ref, f32[4,16,8,128]{3,2,1,0:T(8,128)S(1)} %collective-permute-done.1.above_ref, f32[16,4,8,128]{3,2,1,0:T(8,128)S(1)} %collective-permute-done.2.left_ref, ...), custom_call_target="tpu_custom_call" | custom-call | flops 16777216 | bytes 4194304 | tf_op jit(solution)/shard_map/stencil/pallas_call | solution.py:353
  64.5 0.0 collective-permute-done.13.refs_2_
  64.6 1.1 collective-permute-done.12.refs_0_
  65.7 0.1 collective-permute-start.14
  65.8 1.4 %collective-permute-done.14.refs_1_ = f32[288,72]{1,0:T(8,128)S(1)} collective-permute-done((f32[288,72]{1,0:T(8,128)S(1)}, f32[288,72]{1,0:T(8,128)S(1)}, u32[]{:S(2)}, u32[]{:S(2)}) %collective-permute-start.14) | collective-permute-done | bytes 82976 | tf_op jit(solution)/shard_map/ppermute | solution.py:28
  67.1 23.9 %spread.1 = (f32[2048,128]{1,0:T(8,128)S(1)}, f32[16,128]{1,0:T(8,128)S(1)}, f32[16,128]{1,0:T(8,128)S(1)}) custom-call(f32[288,72]{1,0:T(8,128)S(1)} %stack.3.refs_0_, f32[288,72]{1,0:T(8,128)S(1)} %collective-permute-done.14.refs_1_, s32[1,16384]{1,0:T(1,128)S(1)} %add_bitcast_fusion.code_ref.refs_2_, f32[9,1,16384]{2,1,0:T(1,128)S(1)} %bitcast.20, ...), custom_call_target="tpu_custom_call" | custom-call | flops 17179869184 | bytes 8388608 | tf_op jit(solution)/shard_map/spread/pallas_call | solution.py:483
  91.0 0.2 collective-permute-start.15
  91.2 1.0 collective-permute-done.15.refs_1_
  92.2 14.4 %all_to_all.11 = f32[16,16,128]{2,1,0:T(8,128)S(1)} all-to-all(f32[16,16,128]{2,1,0:T(8,128)S(1)} %bitcast.17), channel_id=1, replica_groups=mesh['gx'=4,'gy'=4,'gz'=2] {'gx','gy'}, dimensions={0} | all-to-all | bytes 262144 | tf_op jit(solution)/shard_map/all_to_all | solution.py:230
  106.6 0.1 collective-permute-start.16
  106.7 1.2 %collective-permute-done.16.refs_1_ = f32[16,128]{1,0:T(8,128)S(1)} collective-permute-done((f32[16,128]{1,0:T(8,128)S(1)}, f32[16,128]{1,0:T(8,128)S(1)}, u32[]{:S(2)}, u32[]{:S(2)}) %collective-permute-start.16) | collective-permute-done | bytes 8224 | tf_op jit(solution)/shard_map/ppermute | solution.py:28
  107.9 5.5 %finish.1 = f32[8,256,128]{2,1,0:T(8,128)} custom-call(f32[2048,128]{1,0:T(8,128)S(1)} %get-tuple-element.80.applied_ref, bf16[64,32768]{1,0:T(8,128)(2,1)S(1)} %get-tuple-element.78.refs_5_.locked_ref, f32[16,128]{1,0:T(8,128)S(1)} %fold.3.refs_0_, f32[16,128]{1,0:T(8,128)S(1)} %collective-permute-done.16.refs_1_), custom_call_target="tpu_custom_call" | custom-call | tf_op jit(solution)/shard_map/finish/pallas_call | solution.py:604
  (18 shorter events, 0.1 us)
Async XLA Ops:
  0.0 1.2 %copy-start.1 = (f32[8,16,16,128]{3,2,1,0:T(8,128)S(1)}, f32[8,16,16,128]{3,2,1,0:T(8,128)}, u32[]{:S(2)}) copy-start(f32[8,16,16,128]{3,2,1,0:T(8,128)} %param.9) | copy-start | bytes 3145732
  2.0 34.1 %collective-permute-start.4 = (f32[16,8,128]{2,1,0:T(8,128)S(1)}, f32[16,8,128]{2,1,0:T(8,128)S(1)}, u32[]{:S(2)}, u32[]{:S(2)}) collective-permute-start(f32[16,8,128]{2,1,0:T(8,128)S(1)} %get-tuple-element.51), channel_id=1, source_target_pairs={{0,1},{1,0},{2,3},{3,2},{4,5},{5,4},{6,7},{7,6},{8,9},{9,8},{10,11... | collective-permute-start | bytes 196616 | tf_op jit(solution)/shard_map/ppermute | solution.py:28
  2.5 33.5 %collective-permute-start = (f32[4,16,8,128]{3,2,1,0:T(8,128)S(1)}, f32[4,16,8,128]{3,2,1,0:T(8,128)S(1)}, u32[]{:S(2)}, u32[]{:S(2)}) collective-permute-start(f32[4,16,8,128]{3,2,1,0:T(8,128)S(1)} %get-tuple-element.47), channel_id=1, source_target_pairs={{0,8},{8,16},{16,24},{24,0},{1,9},{9,17},{17,25},{25,1},{2,10},{10... | collective-permute-start | bytes 786440 | tf_op jit(solution)/shard_map/ppermute | solution.py:28
  5.1 31.0 %collective-permute-start.1 = (f32[4,16,8,128]{3,2,1,0:T(8,128)S(1)}, f32[4,16,8,128]{3,2,1,0:T(8,128)S(1)}, u32[]{:S(2)}, u32[]{:S(2)}) collective-permute-start(f32[4,16,8,128]{3,2,1,0:T(8,128)S(1)} %get-tuple-element.48), channel_id=1, source_target_pairs={{0,24},{8,0},{16,8},{24,16},{1,25},{9,1},{17,9},{25,17},{2,26},{10... | collective-permute-start | bytes 786440 | tf_op jit(solution)/shard_map/ppermute | solution.py:28
  6.1 30.0 %collective-permute-start.2 = (f32[16,4,8,128]{3,2,1,0:T(8,128)S(1)}, f32[16,4,8,128]{3,2,1,0:T(8,128)S(1)}, u32[]{:S(2)}, u32[]{:S(2)}) collective-permute-start(f32[16,4,8,128]{3,2,1,0:T(8,128)S(1)} %get-tuple-element.49), channel_id=1, source_target_pairs={{0,2},{2,4},{4,6},{6,0},{1,3},{3,5},{5,7},{7,1},{8,10},{10,12},{12... | collective-permute-start | bytes 786440 | tf_op jit(solution)/shard_map/ppermute | solution.py:28
  8.1 28.0 %collective-permute-start.3 = (f32[16,4,8,128]{3,2,1,0:T(8,128)S(1)}, f32[16,4,8,128]{3,2,1,0:T(8,128)S(1)}, u32[]{:S(2)}, u32[]{:S(2)}) collective-permute-start(f32[16,4,8,128]{3,2,1,0:T(8,128)S(1)} %get-tuple-element.50), channel_id=1, source_target_pairs={{0,6},{2,0},{4,2},{6,4},{1,7},{3,1},{5,3},{7,5},{8,14},{10,8},{12,... | collective-permute-start | bytes 786440 | tf_op jit(solution)/shard_map/ppermute | solution.py:28
  11.1 1.1 copy-start.3
  12.2 28.3 %copy-start.5 = (f32[1,1,1,32,9]{3,2,4,1,0:T(1,128)S(1)}, f32[1,1,1,32,9]{3,2,4,1,0:T(1,128)}, u32[]{:S(2)}) copy-start(f32[1,1,1,32,9]{3,2,4,1,0:T(1,128)} %param.16) | copy-start | bytes 3460
  12.2 28.3 %copy-start.6 = (s32[1,1,1,32]{3,2,1,0:T(1,128)S(1)}, s32[1,1,1,32]{3,2,1,0:T(1,128)}, u32[]{:S(2)}) copy-start(s32[1,1,1,32]{3,2,1,0:T(1,128)} %param.17) | copy-start | bytes 388
  12.2 54.9 %copy-start.4 = (f32[1,1,1,9,16384]{4,2,3,1,0:T(1,128)S(1)}, f32[1,1,1,9,16384]{4,2,3,1,0:T(1,128)}, u32[]{:S(2)}) copy-start(f32[1,1,1,9,16384]{4,2,3,1,0:T(1,128)} %param.15) | copy-start | bytes 1769476
  36.0 25.0 %copy-start.2 = (f32[16,16,128]{2,1,0:T(8,128)S(1)}, f32[16,16,128]{2,1,0:T(8,128)}, u32[]{:S(2)}) copy-start(f32[16,16,128]{2,1,0:T(8,128)} %pot_ref.1) | copy-start | bytes 393220
  36.1 1.4 %collective-permute-start.5 = (f32[288,72]{1,0:T(8,128)S(1)}, f32[288,72]{1,0:T(8,128)S(1)}, u32[]{:S(2)}, u32[]{:S(2)}) collective-permute-start(f32[288,72]{1,0:T(8,128)S(1)} %get-tuple-element.53), channel_id=1, source_target_pairs={{0,1},{1,0},{2,3},{3,2},{4,5},{5,4},{6,7},{7,6},{8,9},{9,8},{10,11... | collective-permute-start | bytes 248840 | tf_op jit(solution)/shard_map/ppermute | solution.py:28
  37.5 5.3 %collective-permute-start.6 = (f32[96,72]{1,0:T(8,128)S(1)}, f32[96,72]{1,0:T(8,128)S(1)}, u32[]{:S(2)}, u32[]{:S(2)}) collective-permute-start(f32[96,72]{1,0:T(8,128)S(1)} %get-tuple-element.55), channel_id=1, source_target_pairs={{0,8},{8,16},{16,24},{24,0},{1,9},{9,17},{17,25},{25,1},{2,10},{10... | collective-permute-start | bytes 82952 | tf_op jit(solution)/shard_map/ppermute | solution.py:28
  38.4 5.2 %collective-permute-start.7 = (f32[96,72]{1,0:T(8,128)S(1)}, f32[96,72]{1,0:T(8,128)S(1)}, u32[]{:S(2)}, u32[]{:S(2)}) collective-permute-start(f32[96,72]{1,0:T(8,128)S(1)} %get-tuple-element.56), channel_id=1, source_target_pairs={{0,24},{8,0},{16,8},{24,16},{1,25},{9,1},{17,9},{25,17},{2,26},{10... | collective-permute-start | bytes 82952 | tf_op jit(solution)/shard_map/ppermute | solution.py:28
  43.6 5.6 %collective-permute-start.8 = (f32[32,72]{1,0:T(8,128)S(1)}, f32[32,72]{1,0:T(8,128)S(1)}, u32[]{:S(2)}, u32[]{:S(2)}) collective-permute-start(f32[32,72]{1,0:T(8,128)S(1)} %get-tuple-element.58), channel_id=1, source_target_pairs={{0,2},{2,4},{4,6},{6,0},{1,3},{3,5},{5,7},{7,1},{8,10},{10,12},{12... | collective-permute-start | bytes 27656 | tf_op jit(solution)/shard_map/ppermute | solution.py:28
  43.7 5.5 %collective-permute-start.9 = (f32[32,72]{1,0:T(8,128)S(1)}, f32[32,72]{1,0:T(8,128)S(1)}, u32[]{:S(2)}, u32[]{:S(2)}) collective-permute-start(f32[32,72]{1,0:T(8,128)S(1)} %get-tuple-element.59), channel_id=1, source_target_pairs={{0,6},{2,0},{4,2},{6,4},{1,7},{3,1},{5,3},{7,5},{8,14},{10,8},{12,... | collective-permute-start | bytes 27656 | tf_op jit(solution)/shard_map/ppermute | solution.py:28
  49.2 9.5 %collective-permute-start.11 = (f32[32,72]{1,0:T(8,128)S(1)}, f32[32,72]{1,0:T(8,128)S(1)}, u32[]{:S(2)}, u32[]{:S(2)}) collective-permute-start(f32[32,72]{1,0:T(8,128)S(1)} %weigh.1.refs_1_), channel_id=1, source_target_pairs={{0,6},{2,0},{4,2},{6,4},{1,7},{3,1},{5,3},{7,5},{8,14},{10,8},{12,... | collective-permute-start | bytes 27656 | tf_op jit(solution)/shard_map/ppermute | solution.py:28
  53.1 5.6 %collective-permute-start.10 = (f32[32,72]{1,0:T(8,128)S(1)}, f32[32,72]{1,0:T(8,128)S(1)}, u32[]{:S(2)}, u32[]{:S(2)}) collective-permute-start(f32[32,72]{1,0:T(8,128)S(1)} %weigh.1.refs_1_), channel_id=1, source_target_pairs={{0,2},{2,4},{4,6},{6,0},{1,3},{3,5},{5,7},{7,1},{8,10},{10,12},{12... | collective-permute-start | bytes 27656 | tf_op jit(solution)/shard_map/ppermute | solution.py:28
  53.1 2.2 %copy-start = (bf16[64,16,16,128]{3,2,1,0:T(8,128)(2,1)S(1)}, bf16[64,16,16,128]{3,2,1,0:T(8,128)(2,1)}, u32[]{:S(2)}) copy-start(bf16[64,16,16,128]{3,2,1,0:T(8,128)(2,1)} %param.11) | copy-start | bytes 12582916
  58.7 5.8 %collective-permute-start.13 = (f32[96,72]{1,0:T(8,128)S(1)}, f32[96,72]{1,0:T(8,128)S(1)}, u32[]{:S(2)}, u32[]{:S(2)}) collective-permute-start(f32[96,72]{1,0:T(8,128)S(1)} %stack.2.refs_1_), channel_id=1, source_target_pairs={{0,24},{8,0},{16,8},{24,16},{1,25},{9,1},{17,9},{25,17},{2,26},{10... | collective-permute-start | bytes 82952 | tf_op jit(solution)/shard_map/ppermute | solution.py:28
  60.7 5.0 %collective-permute-start.12 = (f32[96,72]{1,0:T(8,128)S(1)}, f32[96,72]{1,0:T(8,128)S(1)}, u32[]{:S(2)}, u32[]{:S(2)}) collective-permute-start(f32[96,72]{1,0:T(8,128)S(1)} %stack.2.refs_1_), channel_id=1, source_target_pairs={{0,8},{8,16},{16,24},{24,0},{1,9},{9,17},{17,25},{25,1},{2,10},{10... | collective-permute-start | bytes 82952 | tf_op jit(solution)/shard_map/ppermute | solution.py:28
  65.7 1.4 %collective-permute-start.14 = (f32[288,72]{1,0:T(8,128)S(1)}, f32[288,72]{1,0:T(8,128)S(1)}, u32[]{:S(2)}, u32[]{:S(2)}) collective-permute-start(f32[288,72]{1,0:T(8,128)S(1)} %stack.3.refs_0_), channel_id=1, source_target_pairs={{0,1},{1,0},{2,3},{3,2},{4,5},{5,4},{6,7},{7,6},{8,9},{9,8},{10,11... | collective-permute-start | bytes 248840 | tf_op jit(solution)/shard_map/ppermute | solution.py:28
  91.0 1.2 %collective-permute-start.15 = (f32[16,128]{1,0:T(8,128)S(1)}, f32[16,128]{1,0:T(8,128)S(1)}, u32[]{:S(2)}, u32[]{:S(2)}) collective-permute-start(f32[16,128]{1,0:T(8,128)S(1)} %get-tuple-element.82), channel_id=1, source_target_pairs={{0,1},{1,0},{2,3},{3,2},{4,5},{5,4},{6,7},{7,6},{8,9},{9,8},{10,11... | collective-permute-start | bytes 24584 | tf_op jit(solution)/shard_map/ppermute | solution.py:28
  106.6 1.2 %collective-permute-start.16 = (f32[16,128]{1,0:T(8,128)S(1)}, f32[16,128]{1,0:T(8,128)S(1)}, u32[]{:S(2)}, u32[]{:S(2)}) collective-permute-start(f32[16,128]{1,0:T(8,128)S(1)} %fold.3.refs_0_), channel_id=1, source_target_pairs={{0,1},{1,0},{2,3},{3,2},{4,5},{5,4},{6,7},{7,6},{8,9},{9,8},{10,11... | collective-permute-start | bytes 24584 | tf_op jit(solution)/shard_map/ppermute | solution.py:28
